TPU v7x, 256 devices: a whole 4x4x8 slice. The times are simulated.
256 devices in a mesh: tm: 8 (over z_hi, core), space: 32 (over z_lo, x, y).
Axes of the slice: x: 4, y: 4, z: 8 (z_hi: 4, z_lo: 2; z = z_hi * 2 + z_lo), core: 2. Of those that a mesh axis runs over, the one named last changes fastest.
Arguments:
- initial: float32 [4, 256, 16, 128], P(None, 'space'), may hold values from -6 to 6
- velocity: float32 [3, 256, 16, 128], P(None, 'space'), may hold values from -0.5 to 0.5
- diffusivity: float32 [256, 16, 128], P('space'), may hold values from 0.1 to 0.6
Outputs:
- final_nodes: float32 [8, 3, 4, 256, 16, 128], P('tm', None, None, 'space')
All inputs are finite; a program needn't handle non-finite values.
Results may differ from a plain program's by a relative error of at most 0.00002.
Values sent between devices are 32-bit elements; how exact they have to be, the bound alone decides.
A program may use at most 64 MiB of HBM per device.

v0:
```python
import jax
import jax.numpy as jnp
from jax import lax
from jax.sharding import PartitionSpec as P

SWEEPS = 2


step_length = 0.25
half_step = 0.125


def padded_2(block, sides, width):
    for axis, dim in sides:
        count = lax.axis_size(axis)
        forward = [(i, i + 1) for i in range(count - 1)]
        backward = [(target, source) for source, target in forward]
        low = lax.ppermute(
            lax.slice_in_dim(block, block.shape[dim] - width, None, axis=dim), axis, forward
        )
        high = lax.ppermute(lax.slice_in_dim(block, 0, width, axis=dim), axis, backward)
        block = jnp.concatenate([low, block, high], axis=dim)
    return block


def shifted(x, axis, by):
    size = lax.axis_size(axis)
    pairs = [(i, i + by) for i in range(size) if 0 <= i + by < size]
    return lax.ppermute(x, axis, pairs)


def stencil(padded, velocity, diffusivity):
    centre = padded[..., 1:-1, :, :]
    x_plus = padded[..., 2:, :, :]
    x_minus = padded[..., :-2, :, :]
    y_plus = jnp.roll(centre, -1, axis=-2)
    y_minus = jnp.roll(centre, 1, axis=-2)
    z_plus = jnp.roll(centre, -1, axis=-1)
    z_minus = jnp.roll(centre, 1, axis=-1)
    laplace = x_plus + x_minus + (y_plus + y_minus) + (z_plus + z_minus) - 6.0 * centre
    transport = (
        velocity[0] * (x_plus - x_minus)
        + velocity[1] * (y_plus - y_minus)
        + velocity[2] * (z_plus - z_minus)
    )
    return diffusivity * laplace - 0.5 * transport


def operate(field, velocity, diffusivity):
    padded = padded_2(field, (("space", 1),), 1)
    return stencil(padded, velocity, diffusivity)


def operate_nodes(nodes, velocity, diffusivity):
    shape = nodes.shape
    flat = nodes.reshape((shape[0] * shape[1],) + shape[2:])
    padded = padded_2(flat, (("space", 1),), 1)
    return stencil(padded, velocity, diffusivity).reshape(shape)


def body(initial, velocity, diffusivity):
    slices = lax.axis_size("tm")
    position = lax.axis_index("tm")
    is_first = position == 0
    nodes = None
    fine_end = None
    for sweep in range(SWEEPS):
        if sweep == 0:
            guess = initial
            for section in range(slices - 1):
                advanced = guess + step_length * operate(guess, velocity, diffusivity)
                guess = jnp.where(section < position, advanced, guess)
            starts = guess
            old_zero = operate(starts, velocity, diffusivity)
            old_one = old_zero
            old_two = old_zero
            start_image = old_zero
        else:
            received = shifted(fine_end, "tm", 1)
            starts = jnp.where(is_first, initial, received)
            olds = operate_nodes(nodes, velocity, diffusivity)
            old_zero = olds[0]
            old_one = olds[1]
            old_two = olds[2]
            start_image = operate(starts, velocity, diffusivity)
        middle = (
            starts
            + half_step * (start_image - old_zero)
            + step_length * (5.0 / 24.0 * old_zero + 1.0 / 3.0 * old_one - 1.0 / 24.0 * old_two)
        )
        middle_image = operate(middle, velocity, diffusivity)
        end_new = (
            middle
            + half_step * (middle_image - old_one)
            + step_length * (-(1.0 / 24.0) * old_zero + 1.0 / 3.0 * old_one + 5.0 / 24.0 * old_two)
        )
        end_image = operate(end_new, velocity, diffusivity)
        forcing = step_length * ((start_image + 4.0 * middle_image + end_image) / 6.0 - start_image)
        ending = jnp.zeros_like(initial)
        coarse = initial
        for section in range(slices):
            arrived = shifted(ending, "tm", 1)
            coarse = jnp.where(is_first, initial, arrived)
            ending = coarse + step_length * operate(coarse, velocity, diffusivity) + forcing
        middle_node = middle + 0.5 * (coarse - starts + (ending - end_new))
        nodes = jnp.stack([coarse, middle_node, ending], axis=0)
        fine_end = end_new
    return nodes[None]


def solution(mesh):
    return jax.shard_map(
        body,
        mesh=mesh,
        in_specs=(
            P(None, "space", None, None),
            P(None, "space", None, None),
            P("space", None, None),
        ),
        out_specs=P("tm", None, None, "space", None, None),
        check_vma=False,
    )
```

profile of v0, /device:TPU:158, one launch (start us, length us, event | category | flops | bytes accessed | tf_op | source)
XLA Modules:
  0.0 533.0 jit_solution(6612942107101772686)
XLA Ops:
  4.8 7.4 %collective-permute-start.4 = (f32[4,1,16,128]{3,2,1,0:T(8,128)S(1)}, f32[4,1,16,128]{3,2,1,0:T(8,128)S(1)}, u32[]{:S(2)}, u32[]{:S(2)}) collective-permute-start(f32[4,1,16,128]{3,2,1,0:T(8,128)S(1)} %get-tuple-element.304), channel_id=1, source_target_pairs={{0,1},{1,2},{2,3},{3,4},{4,5},{5,6},{6,7},{7,8},{8,9},{9,10},{10,1... | collective-permute-start | bytes 98312 | tf_op jit(solution)/shard_map/ppermute | solution.py:18
  16.8 8.1 %collective-permute-start.6 = (f32[4,1,16,128]{3,2,1,0:T(8,128)S(1)}, f32[4,1,16,128]{3,2,1,0:T(8,128)S(1)}, u32[]{:S(2)}, u32[]{:S(2)}) collective-permute-start(f32[4,1,16,128]{3,2,1,0:T(8,128)S(1)} %get-tuple-element.294), channel_id=1, source_target_pairs={{0,1},{1,2},{2,3},{3,4},{4,5},{5,6},{6,7},{7,8},{8,9},{9,10},{10,1... | collective-permute-start | bytes 98312 | tf_op jit(solution)/shard_map/ppermute | solution.py:18
  29.2 8.6 %collective-permute-start.8 = (f32[4,1,16,128]{3,2,1,0:T(8,128)S(1)}, f32[4,1,16,128]{3,2,1,0:T(8,128)S(1)}, u32[]{:S(2)}, u32[]{:S(2)}) collective-permute-start(f32[4,1,16,128]{3,2,1,0:T(8,128)S(1)} %get-tuple-element.284), channel_id=1, source_target_pairs={{0,1},{1,2},{2,3},{3,4},{4,5},{5,6},{6,7},{7,8},{8,9},{9,10},{10,1... | collective-permute-start | bytes 98312 | tf_op jit(solution)/shard_map/ppermute | solution.py:18
  41.9 8.4 %collective-permute-start.10 = (f32[4,1,16,128]{3,2,1,0:T(8,128)S(1)}, f32[4,1,16,128]{3,2,1,0:T(8,128)S(1)}, u32[]{:S(2)}, u32[]{:S(2)}) collective-permute-start(f32[4,1,16,128]{3,2,1,0:T(8,128)S(1)} %get-tuple-element.274), channel_id=1, source_target_pairs={{0,1},{1,2},{2,3},{3,4},{4,5},{5,6},{6,7},{7,8},{8,9},{9,10},{10,1... | collective-permute-start | bytes 98312 | tf_op jit(solution)/shard_map/ppermute | solution.py:18
  54.6 8.4 %collective-permute-start.12 = (f32[4,1,16,128]{3,2,1,0:T(8,128)S(1)}, f32[4,1,16,128]{3,2,1,0:T(8,128)S(1)}, u32[]{:S(2)}, u32[]{:S(2)}) collective-permute-start(f32[4,1,16,128]{3,2,1,0:T(8,128)S(1)} %get-tuple-element.264), channel_id=1, source_target_pairs={{0,1},{1,2},{2,3},{3,4},{4,5},{5,6},{6,7},{7,8},{8,9},{9,10},{10,1... | collective-permute-start | bytes 98312 | tf_op jit(solution)/shard_map/ppermute | solution.py:18
  67.2 8.4 %collective-permute-start.14 = (f32[4,1,16,128]{3,2,1,0:T(8,128)S(1)}, f32[4,1,16,128]{3,2,1,0:T(8,128)S(1)}, u32[]{:S(2)}, u32[]{:S(2)}) collective-permute-start(f32[4,1,16,128]{3,2,1,0:T(8,128)S(1)} %get-tuple-element.254), channel_id=1, source_target_pairs={{0,1},{1,2},{2,3},{3,4},{4,5},{5,6},{6,7},{7,8},{8,9},{9,10},{10,1... | collective-permute-start | bytes 98312 | tf_op jit(solution)/shard_map/ppermute | solution.py:18
  79.8 8.4 %collective-permute-start.16 = (f32[4,1,16,128]{3,2,1,0:T(8,128)S(1)}, f32[4,1,16,128]{3,2,1,0:T(8,128)S(1)}, u32[]{:S(2)}, u32[]{:S(2)}) collective-permute-start(f32[4,1,16,128]{3,2,1,0:T(8,128)S(1)} %get-tuple-element.244), channel_id=1, source_target_pairs={{0,1},{1,2},{2,3},{3,4},{4,5},{5,6},{6,7},{7,8},{8,9},{9,10},{10,1... | collective-permute-start | bytes 98312 | tf_op jit(solution)/shard_map/ppermute | solution.py:18
  90.5 8.4 %collective-permute-start.18 = (f32[4,1,16,128]{3,2,1,0:T(8,128)S(1)}, f32[4,1,16,128]{3,2,1,0:T(8,128)S(1)}, u32[]{:S(2)}, u32[]{:S(2)}) collective-permute-start(f32[4,1,16,128]{3,2,1,0:T(8,128)S(1)} %get-tuple-element.235), channel_id=1, source_target_pairs={{0,1},{1,2},{2,3},{3,4},{4,5},{5,6},{6,7},{7,8},{8,9},{9,10},{10,1... | collective-permute-start | bytes 98312 | tf_op jit(solution)/shard_map/ppermute | solution.py:18
  101.4 7.6 %collective-permute-done.17 = f32[4,1,16,128]{3,2,1,0:T(8,128)S(1)} collective-permute-done((f32[4,1,16,128]{3,2,1,0:T(8,128)S(1)}, f32[4,1,16,128]{3,2,1,0:T(8,128)S(1)}, u32[]{:S(2)}, u32[]{:S(2)}) %collective-permute-start.17) | collective-permute-done | bytes 32800 | tf_op jit(solution)/shard_map/ppermute | solution.py:21
  111.7 3.9 collective-permute-start.19
  115.6 6.1 %collective-permute-start.2 = (f32[4,1,16,128]{3,2,1,0:T(8,128)S(1)}, f32[4,1,16,128]{3,2,1,0:T(8,128)S(1)}, u32[]{:S(2)}, u32[]{:S(2)}) collective-permute-start(f32[4,1,16,128]{3,2,1,0:T(8,128)S(1)} %get-tuple-element.215), channel_id=1, source_target_pairs={{0,1},{1,2},{2,3},{3,4},{4,5},{5,6},{6,7},{7,8},{8,9},{9,10},{10,1... | collective-permute-start | bytes 98312 | tf_op jit(solution)/shard_map/ppermute | solution.py:18
  124.6 8.1 %collective-permute-start.25 = (f32[4,1,16,128]{3,2,1,0:T(8,128)S(1)}, f32[4,1,16,128]{3,2,1,0:T(8,128)S(1)}, u32[]{:S(2)}, u32[]{:S(2)}) collective-permute-start(f32[4,1,16,128]{3,2,1,0:T(8,128)S(1)} %get-tuple-element.205), channel_id=1, source_target_pairs={{0,1},{1,2},{2,3},{3,4},{4,5},{5,6},{6,7},{7,8},{8,9},{9,10},{10,1... | collective-permute-start | bytes 98312 | tf_op jit(solution)/shard_map/ppermute | solution.py:18
  134.7 8.0 %collective-permute-done.24 = f32[4,1,16,128]{3,2,1,0:T(8,128)S(1)} collective-permute-done((f32[4,1,16,128]{3,2,1,0:T(8,128)S(1)}, f32[4,1,16,128]{3,2,1,0:T(8,128)S(1)}, u32[]{:S(2)}, u32[]{:S(2)}) %collective-permute-start.24) | collective-permute-done | bytes 32800 | tf_op jit(solution)/shard_map/ppermute | solution.py:21
  145.3 7.9 %collective-permute-done.26 = f32[4,8,16,128]{3,2,1,0:T(8,128)S(1)} collective-permute-done((f32[4,8,16,128]{3,2,1,0:T(8,128)S(1)}, f32[4,8,16,128]{3,2,1,0:T(8,128)S(1)}, u32[]{:S(2)}, u32[]{:S(2)}) %collective-permute-start.26) | collective-permute-done | bytes 262176 | tf_op jit(solution)/shard_map/ppermute | solution.py:29
  155.5 8.1 %collective-permute-start.28 = (f32[4,1,16,128]{3,2,1,0:T(8,128)S(1)}, f32[4,1,16,128]{3,2,1,0:T(8,128)S(1)}, u32[]{:S(2)}, u32[]{:S(2)}) collective-permute-start(f32[4,1,16,128]{3,2,1,0:T(8,128)S(1)} %get-tuple-element.194), channel_id=1, source_target_pairs={{0,1},{1,2},{2,3},{3,4},{4,5},{5,6},{6,7},{7,8},{8,9},{9,10},{10,1... | collective-permute-start | bytes 98312 | tf_op jit(solution)/shard_map/ppermute | solution.py:18
  168.0 7.9 %collective-permute-done.29 = f32[4,8,16,128]{3,2,1,0:T(8,128)S(1)} collective-permute-done((f32[4,8,16,128]{3,2,1,0:T(8,128)S(1)}, f32[4,8,16,128]{3,2,1,0:T(8,128)S(1)}, u32[]{:S(2)}, u32[]{:S(2)}) %collective-permute-start.29) | collective-permute-done | bytes 262176 | tf_op jit(solution)/shard_map/ppermute | solution.py:29
  178.1 11.2 %collective-permute-start.31 = (f32[4,1,16,128]{3,2,1,0:T(8,128)S(1)}, f32[4,1,16,128]{3,2,1,0:T(8,128)S(1)}, u32[]{:S(2)}, u32[]{:S(2)}) collective-permute-start(f32[4,1,16,128]{3,2,1,0:T(8,128)S(1)} %get-tuple-element.184), channel_id=1, source_target_pairs={{0,1},{1,2},{2,3},{3,4},{4,5},{5,6},{6,7},{7,8},{8,9},{9,10},{10,1... | collective-permute-start | bytes 98312 | tf_op jit(solution)/shard_map/ppermute | solution.py:18
  193.3 10.7 %collective-permute-done.32 = f32[4,8,16,128]{3,2,1,0:T(8,128)S(1)} collective-permute-done((f32[4,8,16,128]{3,2,1,0:T(8,128)S(1)}, f32[4,8,16,128]{3,2,1,0:T(8,128)S(1)}, u32[]{:S(2)}, u32[]{:S(2)}) %collective-permute-start.32) | collective-permute-done | bytes 262176 | tf_op jit(solution)/shard_map/ppermute | solution.py:29
  206.3 8.1 %collective-permute-start.34 = (f32[4,1,16,128]{3,2,1,0:T(8,128)S(1)}, f32[4,1,16,128]{3,2,1,0:T(8,128)S(1)}, u32[]{:S(2)}, u32[]{:S(2)}) collective-permute-start(f32[4,1,16,128]{3,2,1,0:T(8,128)S(1)} %get-tuple-element.174), channel_id=1, source_target_pairs={{0,1},{1,2},{2,3},{3,4},{4,5},{5,6},{6,7},{7,8},{8,9},{9,10},{10,1... | collective-permute-start | bytes 98312 | tf_op jit(solution)/shard_map/ppermute | solution.py:18
  218.3 7.9 %collective-permute-done.35 = f32[4,8,16,128]{3,2,1,0:T(8,128)S(1)} collective-permute-done((f32[4,8,16,128]{3,2,1,0:T(8,128)S(1)}, f32[4,8,16,128]{3,2,1,0:T(8,128)S(1)}, u32[]{:S(2)}, u32[]{:S(2)}) %collective-permute-start.35) | collective-permute-done | bytes 262176 | tf_op jit(solution)/shard_map/ppermute | solution.py:29
  228.5 8.4 %collective-permute-start.37 = (f32[4,1,16,128]{3,2,1,0:T(8,128)S(1)}, f32[4,1,16,128]{3,2,1,0:T(8,128)S(1)}, u32[]{:S(2)}, u32[]{:S(2)}) collective-permute-start(f32[4,1,16,128]{3,2,1,0:T(8,128)S(1)} %get-tuple-element.164), channel_id=1, source_target_pairs={{0,1},{1,2},{2,3},{3,4},{4,5},{5,6},{6,7},{7,8},{8,9},{9,10},{10,1... | collective-permute-start | bytes 98312 | tf_op jit(solution)/shard_map/ppermute | solution.py:18
  241.1 7.7 %collective-permute-done.38 = f32[4,8,16,128]{3,2,1,0:T(8,128)S(1)} collective-permute-done((f32[4,8,16,128]{3,2,1,0:T(8,128)S(1)}, f32[4,8,16,128]{3,2,1,0:T(8,128)S(1)}, u32[]{:S(2)}, u32[]{:S(2)}) %collective-permute-start.38) | collective-permute-done | bytes 262176 | tf_op jit(solution)/shard_map/ppermute | solution.py:29
  251.1 8.6 %collective-permute-start.40 = (f32[4,1,16,128]{3,2,1,0:T(8,128)S(1)}, f32[4,1,16,128]{3,2,1,0:T(8,128)S(1)}, u32[]{:S(2)}, u32[]{:S(2)}) collective-permute-start(f32[4,1,16,128]{3,2,1,0:T(8,128)S(1)} %get-tuple-element.154), channel_id=1, source_target_pairs={{0,1},{1,2},{2,3},{3,4},{4,5},{5,6},{6,7},{7,8},{8,9},{9,10},{10,1... | collective-permute-start | bytes 98312 | tf_op jit(solution)/shard_map/ppermute | solution.py:18
  265.8 5.9 %collective-permute-done.41 = f32[4,8,16,128]{3,2,1,0:T(8,128)S(1)} collective-permute-done((f32[4,8,16,128]{3,2,1,0:T(8,128)S(1)}, f32[4,8,16,128]{3,2,1,0:T(8,128)S(1)}, u32[]{:S(2)}, u32[]{:S(2)}) %collective-permute-start.41) | collective-permute-done | bytes 262176 | tf_op jit(solution)/shard_map/ppermute | solution.py:29
  274.0 8.6 %collective-permute-start.43 = (f32[4,1,16,128]{3,2,1,0:T(8,128)S(1)}, f32[4,1,16,128]{3,2,1,0:T(8,128)S(1)}, u32[]{:S(2)}, u32[]{:S(2)}) collective-permute-start(f32[4,1,16,128]{3,2,1,0:T(8,128)S(1)} %get-tuple-element.144), channel_id=1, source_target_pairs={{0,1},{1,2},{2,3},{3,4},{4,5},{5,6},{6,7},{7,8},{8,9},{9,10},{10,1... | collective-permute-start | bytes 98312 | tf_op jit(solution)/shard_map/ppermute | solution.py:18
  286.5 7.9 %collective-permute-done.44 = f32[4,8,16,128]{3,2,1,0:T(8,128)S(1)} collective-permute-done((f32[4,8,16,128]{3,2,1,0:T(8,128)S(1)}, f32[4,8,16,128]{3,2,1,0:T(8,128)S(1)}, u32[]{:S(2)}, u32[]{:S(2)}) %collective-permute-start.44) | collective-permute-done | bytes 262176 | tf_op jit(solution)/shard_map/ppermute | solution.py:29
  295.2 8.4 %collective-permute-start.46 = (f32[4,1,16,128]{3,2,1,0:T(8,128)S(1)}, f32[4,1,16,128]{3,2,1,0:T(8,128)S(1)}, u32[]{:S(2)}, u32[]{:S(2)}) collective-permute-start(f32[4,1,16,128]{3,2,1,0:T(8,128)S(1)} %get-tuple-element.133), channel_id=1, source_target_pairs={{0,1},{1,2},{2,3},{3,4},{4,5},{5,6},{6,7},{7,8},{8,9},{9,10},{10,1... | collective-permute-start | bytes 98312 | tf_op jit(solution)/shard_map/ppermute | solution.py:18
  305.6 8.1 %collective-permute-start.23 = (f32[4,1,16,128]{3,2,1,0:T(8,128)S(1)}, f32[4,1,16,128]{3,2,1,0:T(8,128)S(1)}, u32[]{:S(2)}, u32[]{:S(2)}) collective-permute-start(f32[4,1,16,128]{3,2,1,0:T(8,128)S(1)} %get-tuple-element.123), channel_id=1, source_target_pairs={{0,1},{1,2},{2,3},{3,4},{4,5},{5,6},{6,7},{7,8},{8,9},{9,10},{10,1... | collective-permute-start | bytes 98312 | tf_op jit(solution)/shard_map/ppermute | solution.py:18
  318.9 8.1 %collective-permute-start.48 = (f32[12,1,16,128]{3,2,1,0:T(8,128)S(1)}, f32[12,1,16,128]{3,2,1,0:T(8,128)S(1)}, u32[]{:S(2)}, u32[]{:S(2)}) collective-permute-start(f32[12,1,16,128]{3,2,1,0:T(8,128)S(1)} %get-tuple-element.22), channel_id=1, source_target_pairs={{0,1},{1,2},{2,3},{3,4},{4,5},{5,6},{6,7},{7,8},{8,9},{9,10},{10,1... | collective-permute-start | bytes 294920 | tf_op jit(solution)/shard_map/ppermute | solution.py:18
  330.9 8.5 %collective-permute-start.50 = (f32[4,1,16,128]{3,2,1,0:T(8,128)S(1)}, f32[4,1,16,128]{3,2,1,0:T(8,128)S(1)}, u32[]{:S(2)}, u32[]{:S(2)}) collective-permute-start(f32[4,1,16,128]{3,2,1,0:T(8,128)S(1)} %get-tuple-element.113), channel_id=1, source_target_pairs={{0,1},{1,2},{2,3},{3,4},{4,5},{5,6},{6,7},{7,8},{8,9},{9,10},{10,1... | collective-permute-start | bytes 98312 | tf_op jit(solution)/shard_map/ppermute | solution.py:18
  341.4 8.1 %collective-permute-done.49 = f32[4,1,16,128]{3,2,1,0:T(8,128)S(1)} collective-permute-done((f32[4,1,16,128]{3,2,1,0:T(8,128)S(1)}, f32[4,1,16,128]{3,2,1,0:T(8,128)S(1)}, u32[]{:S(2)}, u32[]{:S(2)}) %collective-permute-start.49) | collective-permute-done | bytes 32800 | tf_op jit(solution)/shard_map/ppermute | solution.py:21
  352.1 3.9 collective-permute-start.51
  356.1 6.1 %collective-permute-done.51 = f32[4,1,16,128]{3,2,1,0:T(8,128)S(1)} collective-permute-done((f32[4,1,16,128]{3,2,1,0:T(8,128)S(1)}, f32[4,1,16,128]{3,2,1,0:T(8,128)S(1)}, u32[]{:S(2)}, u32[]{:S(2)}) %collective-permute-start.51) | collective-permute-done | bytes 32800 | tf_op jit(solution)/shard_map/ppermute | solution.py:21
  364.5 9.4 %collective-permute-done.53 = f32[4,8,16,128]{3,2,1,0:T(8,128)S(1)} collective-permute-done((f32[4,8,16,128]{3,2,1,0:T(8,128)S(1)}, f32[4,8,16,128]{3,2,1,0:T(8,128)S(1)}, u32[]{:S(2)}, u32[]{:S(2)}) %collective-permute-start.53) | collective-permute-done | bytes 262176 | tf_op jit(solution)/shard_map/ppermute | solution.py:29
  376.2 8.1 %collective-permute-start.55 = (f32[4,1,16,128]{3,2,1,0:T(8,128)S(1)}, f32[4,1,16,128]{3,2,1,0:T(8,128)S(1)}, u32[]{:S(2)}, u32[]{:S(2)}) collective-permute-start(f32[4,1,16,128]{3,2,1,0:T(8,128)S(1)} %get-tuple-element.92), channel_id=1, source_target_pairs={{0,1},{1,2},{2,3},{3,4},{4,5},{5,6},{6,7},{7,8},{8,9},{9,10},{10,1... | collective-permute-start | bytes 98312 | tf_op jit(solution)/shard_map/ppermute | solution.py:18
  388.2 7.9 %collective-permute-done.56 = f32[4,8,16,128]{3,2,1,0:T(8,128)S(1)} collective-permute-done((f32[4,8,16,128]{3,2,1,0:T(8,128)S(1)}, f32[4,8,16,128]{3,2,1,0:T(8,128)S(1)}, u32[]{:S(2)}, u32[]{:S(2)}) %collective-permute-start.56) | collective-permute-done | bytes 262176 | tf_op jit(solution)/shard_map/ppermute | solution.py:29
  398.4 8.4 %collective-permute-start.58 = (f32[4,1,16,128]{3,2,1,0:T(8,128)S(1)}, f32[4,1,16,128]{3,2,1,0:T(8,128)S(1)}, u32[]{:S(2)}, u32[]{:S(2)}) collective-permute-start(f32[4,1,16,128]{3,2,1,0:T(8,128)S(1)} %get-tuple-element.82), channel_id=1, source_target_pairs={{0,1},{1,2},{2,3},{3,4},{4,5},{5,6},{6,7},{7,8},{8,9},{9,10},{10,1... | collective-permute-start | bytes 98312 | tf_op jit(solution)/shard_map/ppermute | solution.py:18
  410.7 10.7 %collective-permute-done.59 = f32[4,8,16,128]{3,2,1,0:T(8,128)S(1)} collective-permute-done((f32[4,8,16,128]{3,2,1,0:T(8,128)S(1)}, f32[4,8,16,128]{3,2,1,0:T(8,128)S(1)}, u32[]{:S(2)}, u32[]{:S(2)}) %collective-permute-start.59) | collective-permute-done | bytes 262176 | tf_op jit(solution)/shard_map/ppermute | solution.py:29
  423.7 8.1 %collective-permute-start.61 = (f32[4,1,16,128]{3,2,1,0:T(8,128)S(1)}, f32[4,1,16,128]{3,2,1,0:T(8,128)S(1)}, u32[]{:S(2)}, u32[]{:S(2)}) collective-permute-start(f32[4,1,16,128]{3,2,1,0:T(8,128)S(1)} %get-tuple-element.72), channel_id=1, source_target_pairs={{0,1},{1,2},{2,3},{3,4},{4,5},{5,6},{6,7},{7,8},{8,9},{9,10},{10,1... | collective-permute-start | bytes 98312 | tf_op jit(solution)/shard_map/ppermute | solution.py:18
  435.6 7.9 %collective-permute-done.62 = f32[4,8,16,128]{3,2,1,0:T(8,128)S(1)} collective-permute-done((f32[4,8,16,128]{3,2,1,0:T(8,128)S(1)}, f32[4,8,16,128]{3,2,1,0:T(8,128)S(1)}, u32[]{:S(2)}, u32[]{:S(2)}) %collective-permute-start.62) | collective-permute-done | bytes 262176 | tf_op jit(solution)/shard_map/ppermute | solution.py:29
  445.8 8.4 %collective-permute-start.64 = (f32[4,1,16,128]{3,2,1,0:T(8,128)S(1)}, f32[4,1,16,128]{3,2,1,0:T(8,128)S(1)}, u32[]{:S(2)}, u32[]{:S(2)}) collective-permute-start(f32[4,1,16,128]{3,2,1,0:T(8,128)S(1)} %get-tuple-element.62), channel_id=1, source_target_pairs={{0,1},{1,2},{2,3},{3,4},{4,5},{5,6},{6,7},{7,8},{8,9},{9,10},{10,1... | collective-permute-start | bytes 98312 | tf_op jit(solution)/shard_map/ppermute | solution.py:18
  458.4 9.8 %collective-permute-done.65 = f32[4,8,16,128]{3,2,1,0:T(8,128)S(1)} collective-permute-done((f32[4,8,16,128]{3,2,1,0:T(8,128)S(1)}, f32[4,8,16,128]{3,2,1,0:T(8,128)S(1)}, u32[]{:S(2)}, u32[]{:S(2)}) %collective-permute-start.65) | collective-permute-done | bytes 262176 | tf_op jit(solution)/shard_map/ppermute | solution.py:29
  470.5 8.1 %collective-permute-start.67 = (f32[4,1,16,128]{3,2,1,0:T(8,128)S(1)}, f32[4,1,16,128]{3,2,1,0:T(8,128)S(1)}, u32[]{:S(2)}, u32[]{:S(2)}) collective-permute-start(f32[4,1,16,128]{3,2,1,0:T(8,128)S(1)} %get-tuple-element.52), channel_id=1, source_target_pairs={{0,1},{1,2},{2,3},{3,4},{4,5},{5,6},{6,7},{7,8},{8,9},{9,10},{10,1... | collective-permute-start | bytes 98312 | tf_op jit(solution)/shard_map/ppermute | solution.py:18
  482.5 7.9 %collective-permute-done.68 = f32[4,8,16,128]{3,2,1,0:T(8,128)S(1)} collective-permute-done((f32[4,8,16,128]{3,2,1,0:T(8,128)S(1)}, f32[4,8,16,128]{3,2,1,0:T(8,128)S(1)}, u32[]{:S(2)}, u32[]{:S(2)}) %collective-permute-start.68) | collective-permute-done | bytes 262176 | tf_op jit(solution)/shard_map/ppermute | solution.py:29
  492.7 8.4 %collective-permute-start.70 = (f32[4,1,16,128]{3,2,1,0:T(8,128)S(1)}, f32[4,1,16,128]{3,2,1,0:T(8,128)S(1)}, u32[]{:S(2)}, u32[]{:S(2)}) collective-permute-start(f32[4,1,16,128]{3,2,1,0:T(8,128)S(1)} %get-tuple-element.42), channel_id=1, source_target_pairs={{0,1},{1,2},{2,3},{3,4},{4,5},{5,6},{6,7},{7,8},{8,9},{9,10},{10,1... | collective-permute-start | bytes 98312 | tf_op jit(solution)/shard_map/ppermute | solution.py:18
  505.0 7.9 %collective-permute-done.71 = f32[4,8,16,128]{3,2,1,0:T(8,128)S(1)} collective-permute-done((f32[4,8,16,128]{3,2,1,0:T(8,128)S(1)}, f32[4,8,16,128]{3,2,1,0:T(8,128)S(1)}, u32[]{:S(2)}, u32[]{:S(2)}) %collective-permute-start.71) | collective-permute-done | bytes 262176 | tf_op jit(solution)/shard_map/ppermute | solution.py:29
  513.2 8.4 %collective-permute-start.73 = (f32[4,1,16,128]{3,2,1,0:T(8,128)S(1)}, f32[4,1,16,128]{3,2,1,0:T(8,128)S(1)}, u32[]{:S(2)}, u32[]{:S(2)}) collective-permute-start(f32[4,1,16,128]{3,2,1,0:T(8,128)S(1)} %get-tuple-element.33), channel_id=1, source_target_pairs={{0,1},{1,2},{2,3},{3,4},{4,5},{5,6},{6,7},{7,8},{8,9},{9,10},{10,1... | collective-permute-start | bytes 98312 | tf_op jit(solution)/shard_map/ppermute | solution.py:18
  523.6 8.1 %collective-permute-done.72 = f32[4,1,16,128]{3,2,1,0:T(8,128)S(1)} collective-permute-done((f32[4,1,16,128]{3,2,1,0:T(8,128)S(1)}, f32[4,1,16,128]{3,2,1,0:T(8,128)S(1)}, u32[]{:S(2)}, u32[]{:S(2)}) %collective-permute-start.72) | collective-permute-done | bytes 32800 | tf_op jit(solution)/shard_map/ppermute | solution.py:21
  (298 shorter events, 142.8 us)
Async XLA Ops:
  0.0 100.9 %collective-permute-start = (f32[4,8,16,128]{3,2,1,0:T(8,128)S(1)}, f32[4,8,16,128]{3,2,1,0:T(8,128)S(1)}, u32[]{:S(2)}, u32[]{:S(2)}) collective-permute-start(f32[4,8,16,128]{3,2,1,0:T(8,128)S(1)} %broadcast.35), channel_id=1, source_target_pairs={{0,32},{32,64},{64,96},{96,128},{128,160},{160,192},{192,224},{1,3... | collective-permute-start | bytes 786440 | tf_op jit(solution)/shard_map/ppermute | solution.py:29
  2.1 11.4 %collective-permute-start.3 = (f32[4,1,16,128]{3,2,1,0:T(8,128)S(1)}, f32[4,1,16,128]{3,2,1,0:T(8,128)S(1)}, u32[]{:S(2)}, u32[]{:S(2)}) collective-permute-start(f32[4,1,16,128]{3,2,1,0:T(8,128)S(1)} %get-tuple-element.305), channel_id=1, source_target_pairs={{1,0},{2,1},{3,2},{4,3},{5,4},{6,5},{7,6},{8,7},{9,8},{10,9},{11,1... | collective-permute-start | bytes 98312 | tf_op jit(solution)/shard_map/ppermute | solution.py:21
  14.9 10.3 %collective-permute-start.5 = (f32[4,1,16,128]{3,2,1,0:T(8,128)S(1)}, f32[4,1,16,128]{3,2,1,0:T(8,128)S(1)}, u32[]{:S(2)}, u32[]{:S(2)}) collective-permute-start(f32[4,1,16,128]{3,2,1,0:T(8,128)S(1)} %get-tuple-element.295), channel_id=1, source_target_pairs={{1,0},{2,1},{3,2},{4,3},{5,4},{6,5},{7,6},{8,7},{9,8},{10,9},{11,1... | collective-permute-start | bytes 98312 | tf_op jit(solution)/shard_map/ppermute | solution.py:21
  27.2 10.5 %collective-permute-start.7 = (f32[4,1,16,128]{3,2,1,0:T(8,128)S(1)}, f32[4,1,16,128]{3,2,1,0:T(8,128)S(1)}, u32[]{:S(2)}, u32[]{:S(2)}) collective-permute-start(f32[4,1,16,128]{3,2,1,0:T(8,128)S(1)} %get-tuple-element.285), channel_id=1, source_target_pairs={{1,0},{2,1},{3,2},{4,3},{5,4},{6,5},{7,6},{8,7},{9,8},{10,9},{11,1... | collective-permute-start | bytes 98312 | tf_op jit(solution)/shard_map/ppermute | solution.py:21
  29.2 10.1 %collective-permute-start.8 = (f32[4,1,16,128]{3,2,1,0:T(8,128)S(1)}, f32[4,1,16,128]{3,2,1,0:T(8,128)S(1)}, u32[]{:S(2)}, u32[]{:S(2)}) collective-permute-start(f32[4,1,16,128]{3,2,1,0:T(8,128)S(1)} %get-tuple-element.284), channel_id=1, source_target_pairs={{0,1},{1,2},{2,3},{3,4},{4,5},{5,6},{6,7},{7,8},{8,9},{9,10},{10,1... | collective-permute-start | bytes 98312 | tf_op jit(solution)/shard_map/ppermute | solution.py:18
  40.0 10.4 %collective-permute-start.9 = (f32[4,1,16,128]{3,2,1,0:T(8,128)S(1)}, f32[4,1,16,128]{3,2,1,0:T(8,128)S(1)}, u32[]{:S(2)}, u32[]{:S(2)}) collective-permute-start(f32[4,1,16,128]{3,2,1,0:T(8,128)S(1)} %get-tuple-element.275), channel_id=1, source_target_pairs={{1,0},{2,1},{3,2},{4,3},{5,4},{6,5},{7,6},{8,7},{9,8},{10,9},{11,1... | collective-permute-start | bytes 98312 | tf_op jit(solution)/shard_map/ppermute | solution.py:21
  52.6 10.4 %collective-permute-start.11 = (f32[4,1,16,128]{3,2,1,0:T(8,128)S(1)}, f32[4,1,16,128]{3,2,1,0:T(8,128)S(1)}, u32[]{:S(2)}, u32[]{:S(2)}) collective-permute-start(f32[4,1,16,128]{3,2,1,0:T(8,128)S(1)} %get-tuple-element.265), channel_id=1, source_target_pairs={{1,0},{2,1},{3,2},{4,3},{5,4},{6,5},{7,6},{8,7},{9,8},{10,9},{11,1... | collective-permute-start | bytes 98312 | tf_op jit(solution)/shard_map/ppermute | solution.py:21
  65.3 10.4 %collective-permute-start.13 = (f32[4,1,16,128]{3,2,1,0:T(8,128)S(1)}, f32[4,1,16,128]{3,2,1,0:T(8,128)S(1)}, u32[]{:S(2)}, u32[]{:S(2)}) collective-permute-start(f32[4,1,16,128]{3,2,1,0:T(8,128)S(1)} %get-tuple-element.255), channel_id=1, source_target_pairs={{1,0},{2,1},{3,2},{4,3},{5,4},{6,5},{7,6},{8,7},{9,8},{10,9},{11,1... | collective-permute-start | bytes 98312 | tf_op jit(solution)/shard_map/ppermute | solution.py:21
  77.9 10.4 %collective-permute-start.15 = (f32[4,1,16,128]{3,2,1,0:T(8,128)S(1)}, f32[4,1,16,128]{3,2,1,0:T(8,128)S(1)}, u32[]{:S(2)}, u32[]{:S(2)}) collective-permute-start(f32[4,1,16,128]{3,2,1,0:T(8,128)S(1)} %get-tuple-element.245), channel_id=1, source_target_pairs={{1,0},{2,1},{3,2},{4,3},{5,4},{6,5},{7,6},{8,7},{9,8},{10,9},{11,1... | collective-permute-start | bytes 98312 | tf_op jit(solution)/shard_map/ppermute | solution.py:21
  90.5 10.8 %collective-permute-start.18 = (f32[4,1,16,128]{3,2,1,0:T(8,128)S(1)}, f32[4,1,16,128]{3,2,1,0:T(8,128)S(1)}, u32[]{:S(2)}, u32[]{:S(2)}) collective-permute-start(f32[4,1,16,128]{3,2,1,0:T(8,128)S(1)} %get-tuple-element.235), channel_id=1, source_target_pairs={{0,1},{1,2},{2,3},{3,4},{4,5},{5,6},{6,7},{7,8},{8,9},{9,10},{10,1... | collective-permute-start | bytes 98312 | tf_op jit(solution)/shard_map/ppermute | solution.py:18
  109.8 14.0 %collective-permute-start.20 = (f32[4,1,16,128]{3,2,1,0:T(8,128)S(1)}, f32[4,1,16,128]{3,2,1,0:T(8,128)S(1)}, u32[]{:S(2)}, u32[]{:S(2)}) collective-permute-start(f32[4,1,16,128]{3,2,1,0:T(8,128)S(1)} %get-tuple-element.225), channel_id=1, source_target_pairs={{0,1},{1,2},{2,3},{3,4},{4,5},{5,6},{6,7},{7,8},{8,9},{9,10},{10,1... | collective-permute-start | bytes 98312 | tf_op jit(solution)/shard_map/ppermute | solution.py:18
  111.7 12.0 %collective-permute-start.19 = (f32[4,1,16,128]{3,2,1,0:T(8,128)S(1)}, f32[4,1,16,128]{3,2,1,0:T(8,128)S(1)}, u32[]{:S(2)}, u32[]{:S(2)}) collective-permute-start(f32[4,1,16,128]{3,2,1,0:T(8,128)S(1)} %get-tuple-element.224), channel_id=1, source_target_pairs={{1,0},{2,1},{3,2},{4,3},{5,4},{6,5},{7,6},{8,7},{9,8},{10,9},{11,1... | collective-permute-start | bytes 98312 | tf_op jit(solution)/shard_map/ppermute | solution.py:21
  115.6 19.0 %collective-permute-start.2 = (f32[4,1,16,128]{3,2,1,0:T(8,128)S(1)}, f32[4,1,16,128]{3,2,1,0:T(8,128)S(1)}, u32[]{:S(2)}, u32[]{:S(2)}) collective-permute-start(f32[4,1,16,128]{3,2,1,0:T(8,128)S(1)} %get-tuple-element.215), channel_id=1, source_target_pairs={{0,1},{1,2},{2,3},{3,4},{4,5},{5,6},{6,7},{7,8},{8,9},{9,10},{10,1... | collective-permute-start | bytes 98312 | tf_op jit(solution)/shard_map/ppermute | solution.py:18
  121.8 12.9 %collective-permute-start.1 = (f32[4,1,16,128]{3,2,1,0:T(8,128)S(1)}, f32[4,1,16,128]{3,2,1,0:T(8,128)S(1)}, u32[]{:S(2)}, u32[]{:S(2)}) collective-permute-start(f32[4,1,16,128]{3,2,1,0:T(8,128)S(1)} %get-tuple-element.214), channel_id=1, source_target_pairs={{1,0},{2,1},{3,2},{4,3},{5,4},{6,5},{7,6},{8,7},{9,8},{10,9},{11,1... | collective-permute-start | bytes 98312 | tf_op jit(solution)/shard_map/ppermute | solution.py:21
  124.6 10.1 %collective-permute-start.25 = (f32[4,1,16,128]{3,2,1,0:T(8,128)S(1)}, f32[4,1,16,128]{3,2,1,0:T(8,128)S(1)}, u32[]{:S(2)}, u32[]{:S(2)}) collective-permute-start(f32[4,1,16,128]{3,2,1,0:T(8,128)S(1)} %get-tuple-element.205), channel_id=1, source_target_pairs={{0,1},{1,2},{2,3},{3,4},{4,5},{5,6},{6,7},{7,8},{8,9},{9,10},{10,1... | collective-permute-start | bytes 98312 | tf_op jit(solution)/shard_map/ppermute | solution.py:18
  153.6 10.1 %collective-permute-start.27 = (f32[4,1,16,128]{3,2,1,0:T(8,128)S(1)}, f32[4,1,16,128]{3,2,1,0:T(8,128)S(1)}, u32[]{:S(2)}, u32[]{:S(2)}) collective-permute-start(f32[4,1,16,128]{3,2,1,0:T(8,128)S(1)} %get-tuple-element.195), channel_id=1, source_target_pairs={{1,0},{2,1},{3,2},{4,3},{5,4},{6,5},{7,6},{8,7},{9,8},{10,9},{11,1... | collective-permute-start | bytes 98312 | tf_op jit(solution)/shard_map/ppermute | solution.py:21
  155.5 10.2 %collective-permute-start.28 = (f32[4,1,16,128]{3,2,1,0:T(8,128)S(1)}, f32[4,1,16,128]{3,2,1,0:T(8,128)S(1)}, u32[]{:S(2)}, u32[]{:S(2)}) collective-permute-start(f32[4,1,16,128]{3,2,1,0:T(8,128)S(1)} %get-tuple-element.194), channel_id=1, source_target_pairs={{0,1},{1,2},{2,3},{3,4},{4,5},{5,6},{6,7},{7,8},{8,9},{9,10},{10,1... | collective-permute-start | bytes 98312 | tf_op jit(solution)/shard_map/ppermute | solution.py:18
  176.2 13.2 %collective-permute-start.30 = (f32[4,1,16,128]{3,2,1,0:T(8,128)S(1)}, f32[4,1,16,128]{3,2,1,0:T(8,128)S(1)}, u32[]{:S(2)}, u32[]{:S(2)}) collective-permute-start(f32[4,1,16,128]{3,2,1,0:T(8,128)S(1)} %get-tuple-element.185), channel_id=1, source_target_pairs={{1,0},{2,1},{3,2},{4,3},{5,4},{6,5},{7,6},{8,7},{9,8},{10,9},{11,1... | collective-permute-start | bytes 98312 | tf_op jit(solution)/shard_map/ppermute | solution.py:21
  178.1 12.9 %collective-permute-start.31 = (f32[4,1,16,128]{3,2,1,0:T(8,128)S(1)}, f32[4,1,16,128]{3,2,1,0:T(8,128)S(1)}, u32[]{:S(2)}, u32[]{:S(2)}) collective-permute-start(f32[4,1,16,128]{3,2,1,0:T(8,128)S(1)} %get-tuple-element.184), channel_id=1, source_target_pairs={{0,1},{1,2},{2,3},{3,4},{4,5},{5,6},{6,7},{7,8},{8,9},{9,10},{10,1... | collective-permute-start | bytes 98312 | tf_op jit(solution)/shard_map/ppermute | solution.py:18
  191.4 12.6 %collective-permute-start.32 = (f32[4,8,16,128]{3,2,1,0:T(8,128)S(1)}, f32[4,8,16,128]{3,2,1,0:T(8,128)S(1)}, u32[]{:S(2)}, u32[]{:S(2)}) collective-permute-start(f32[4,8,16,128]{3,2,1,0:T(8,128)S(1)} %add_add_fusion.12), channel_id=1, source_target_pairs={{0,32},{32,64},{64,96},{96,128},{128,160},{160,192},{192,224},{1,3... | collective-permute-start | bytes 786440 | tf_op jit(solution)/shard_map/ppermute | solution.py:29
  204.4 10.1 %collective-permute-start.33 = (f32[4,1,16,128]{3,2,1,0:T(8,128)S(1)}, f32[4,1,16,128]{3,2,1,0:T(8,128)S(1)}, u32[]{:S(2)}, u32[]{:S(2)}) collective-permute-start(f32[4,1,16,128]{3,2,1,0:T(8,128)S(1)} %get-tuple-element.175), channel_id=1, source_target_pairs={{1,0},{2,1},{3,2},{4,3},{5,4},{6,5},{7,6},{8,7},{9,8},{10,9},{11,1... | collective-permute-start | bytes 98312 | tf_op jit(solution)/shard_map/ppermute | solution.py:21
  226.6 10.4 %collective-permute-start.36 = (f32[4,1,16,128]{3,2,1,0:T(8,128)S(1)}, f32[4,1,16,128]{3,2,1,0:T(8,128)S(1)}, u32[]{:S(2)}, u32[]{:S(2)}) collective-permute-start(f32[4,1,16,128]{3,2,1,0:T(8,128)S(1)} %get-tuple-element.165), channel_id=1, source_target_pairs={{1,0},{2,1},{3,2},{4,3},{5,4},{6,5},{7,6},{8,7},{9,8},{10,9},{11,1... | collective-permute-start | bytes 98312 | tf_op jit(solution)/shard_map/ppermute | solution.py:21
  228.5 10.2 %collective-permute-start.37 = (f32[4,1,16,128]{3,2,1,0:T(8,128)S(1)}, f32[4,1,16,128]{3,2,1,0:T(8,128)S(1)}, u32[]{:S(2)}, u32[]{:S(2)}) collective-permute-start(f32[4,1,16,128]{3,2,1,0:T(8,128)S(1)} %get-tuple-element.164), channel_id=1, source_target_pairs={{0,1},{1,2},{2,3},{3,4},{4,5},{5,6},{6,7},{7,8},{8,9},{9,10},{10,1... | collective-permute-start | bytes 98312 | tf_op jit(solution)/shard_map/ppermute | solution.py:18
  249.2 10.6 %collective-permute-start.39 = (f32[4,1,16,128]{3,2,1,0:T(8,128)S(1)}, f32[4,1,16,128]{3,2,1,0:T(8,128)S(1)}, u32[]{:S(2)}, u32[]{:S(2)}) collective-permute-start(f32[4,1,16,128]{3,2,1,0:T(8,128)S(1)} %get-tuple-element.155), channel_id=1, source_target_pairs={{1,0},{2,1},{3,2},{4,3},{5,4},{6,5},{7,6},{8,7},{9,8},{10,9},{11,1... | collective-permute-start | bytes 98312 | tf_op jit(solution)/shard_map/ppermute | solution.py:21
  251.1 10.4 %collective-permute-start.40 = (f32[4,1,16,128]{3,2,1,0:T(8,128)S(1)}, f32[4,1,16,128]{3,2,1,0:T(8,128)S(1)}, u32[]{:S(2)}, u32[]{:S(2)}) collective-permute-start(f32[4,1,16,128]{3,2,1,0:T(8,128)S(1)} %get-tuple-element.154), channel_id=1, source_target_pairs={{0,1},{1,2},{2,3},{3,4},{4,5},{5,6},{6,7},{7,8},{8,9},{9,10},{10,1... | collective-permute-start | bytes 98312 | tf_op jit(solution)/shard_map/ppermute | solution.py:18
  263.9 22.7 %collective-permute-start.21 = (f32[4,8,16,128]{3,2,1,0:T(8,128)S(1)}, f32[4,8,16,128]{3,2,1,0:T(8,128)S(1)}, u32[]{:S(2)}, u32[]{:S(2)}) collective-permute-start(f32[4,8,16,128]{3,2,1,0:T(8,128)S(1)} %get-tuple-element.18), channel_id=1, source_target_pairs={{0,32},{32,64},{64,96},{96,128},{128,160},{160,192},{192,224},{1,3... | collective-permute-start | bytes 786440 | tf_op jit(solution)/shard_map/ppermute | solution.py:29
  272.1 10.6 %collective-permute-start.42 = (f32[4,1,16,128]{3,2,1,0:T(8,128)S(1)}, f32[4,1,16,128]{3,2,1,0:T(8,128)S(1)}, u32[]{:S(2)}, u32[]{:S(2)}) collective-permute-start(f32[4,1,16,128]{3,2,1,0:T(8,128)S(1)} %get-tuple-element.145), channel_id=1, source_target_pairs={{1,0},{2,1},{3,2},{4,3},{5,4},{6,5},{7,6},{8,7},{9,8},{10,9},{11,1... | collective-permute-start | bytes 98312 | tf_op jit(solution)/shard_map/ppermute | solution.py:21
  274.0 10.2 %collective-permute-start.43 = (f32[4,1,16,128]{3,2,1,0:T(8,128)S(1)}, f32[4,1,16,128]{3,2,1,0:T(8,128)S(1)}, u32[]{:S(2)}, u32[]{:S(2)}) collective-permute-start(f32[4,1,16,128]{3,2,1,0:T(8,128)S(1)} %get-tuple-element.144), channel_id=1, source_target_pairs={{0,1},{1,2},{2,3},{3,4},{4,5},{5,6},{6,7},{7,8},{8,9},{9,10},{10,1... | collective-permute-start | bytes 98312 | tf_op jit(solution)/shard_map/ppermute | solution.py:18
  295.2 20.5 %collective-permute-start.46 = (f32[4,1,16,128]{3,2,1,0:T(8,128)S(1)}, f32[4,1,16,128]{3,2,1,0:T(8,128)S(1)}, u32[]{:S(2)}, u32[]{:S(2)}) collective-permute-start(f32[4,1,16,128]{3,2,1,0:T(8,128)S(1)} %get-tuple-element.133), channel_id=1, source_target_pairs={{0,1},{1,2},{2,3},{3,4},{4,5},{5,6},{6,7},{7,8},{8,9},{9,10},{10,1... | collective-permute-start | bytes 98312 | tf_op jit(solution)/shard_map/ppermute | solution.py:18
  303.6 12.0 %collective-permute-start.45 = (f32[4,1,16,128]{3,2,1,0:T(8,128)S(1)}, f32[4,1,16,128]{3,2,1,0:T(8,128)S(1)}, u32[]{:S(2)}, u32[]{:S(2)}) collective-permute-start(f32[4,1,16,128]{3,2,1,0:T(8,128)S(1)} %get-tuple-element.132), channel_id=1, source_target_pairs={{1,0},{2,1},{3,2},{4,3},{5,4},{6,5},{7,6},{8,7},{9,8},{10,9},{11,1... | collective-permute-start | bytes 98312 | tf_op jit(solution)/shard_map/ppermute | solution.py:21
  305.6 24.6 %collective-permute-start.23 = (f32[4,1,16,128]{3,2,1,0:T(8,128)S(1)}, f32[4,1,16,128]{3,2,1,0:T(8,128)S(1)}, u32[]{:S(2)}, u32[]{:S(2)}) collective-permute-start(f32[4,1,16,128]{3,2,1,0:T(8,128)S(1)} %get-tuple-element.123), channel_id=1, source_target_pairs={{0,1},{1,2},{2,3},{3,4},{4,5},{5,6},{6,7},{7,8},{8,9},{9,10},{10,1... | collective-permute-start | bytes 98312 | tf_op jit(solution)/shard_map/ppermute | solution.py:18
  313.7 16.4 %collective-permute-start.22 = (f32[4,1,16,128]{3,2,1,0:T(8,128)S(1)}, f32[4,1,16,128]{3,2,1,0:T(8,128)S(1)}, u32[]{:S(2)}, u32[]{:S(2)}) collective-permute-start(f32[4,1,16,128]{3,2,1,0:T(8,128)S(1)} %get-tuple-element.122), channel_id=1, source_target_pairs={{1,0},{2,1},{3,2},{4,3},{5,4},{6,5},{7,6},{8,7},{9,8},{10,9},{11,1... | collective-permute-start | bytes 98312 | tf_op jit(solution)/shard_map/ppermute | solution.py:21
  317.0 10.7 %collective-permute-start.47 = (f32[12,1,16,128]{3,2,1,0:T(8,128)S(1)}, f32[12,1,16,128]{3,2,1,0:T(8,128)S(1)}, u32[]{:S(2)}, u32[]{:S(2)}) collective-permute-start(f32[12,1,16,128]{3,2,1,0:T(8,128)S(1)} %get-tuple-element.23), channel_id=1, source_target_pairs={{1,0},{2,1},{3,2},{4,3},{5,4},{6,5},{7,6},{8,7},{9,8},{10,9},{11,1... | collective-permute-start | bytes 294920 | tf_op jit(solution)/shard_map/ppermute | solution.py:21
  318.9 10.3 %collective-permute-start.48 = (f32[12,1,16,128]{3,2,1,0:T(8,128)S(1)}, f32[12,1,16,128]{3,2,1,0:T(8,128)S(1)}, u32[]{:S(2)}, u32[]{:S(2)}) collective-permute-start(f32[12,1,16,128]{3,2,1,0:T(8,128)S(1)} %get-tuple-element.22), channel_id=1, source_target_pairs={{0,1},{1,2},{2,3},{3,4},{4,5},{5,6},{6,7},{7,8},{8,9},{9,10},{10,1... | collective-permute-start | bytes 294920 | tf_op jit(solution)/shard_map/ppermute | solution.py:18
  330.9 10.5 %collective-permute-start.50 = (f32[4,1,16,128]{3,2,1,0:T(8,128)S(1)}, f32[4,1,16,128]{3,2,1,0:T(8,128)S(1)}, u32[]{:S(2)}, u32[]{:S(2)}) collective-permute-start(f32[4,1,16,128]{3,2,1,0:T(8,128)S(1)} %get-tuple-element.113), channel_id=1, source_target_pairs={{0,1},{1,2},{2,3},{3,4},{4,5},{5,6},{6,7},{7,8},{8,9},{9,10},{10,1... | collective-permute-start | bytes 98312 | tf_op jit(solution)/shard_map/ppermute | solution.py:18
  362.5 11.4 %collective-permute-start.53 = (f32[4,8,16,128]{3,2,1,0:T(8,128)S(1)}, f32[4,8,16,128]{3,2,1,0:T(8,128)S(1)}, u32[]{:S(2)}, u32[]{:S(2)}) collective-permute-start(f32[4,8,16,128]{3,2,1,0:T(8,128)S(1)} %get-tuple-element.7), channel_id=1, source_target_pairs={{0,32},{32,64},{64,96},{96,128},{128,160},{160,192},{192,224},{1,3... | collective-permute-start | bytes 786440 | tf_op jit(solution)/shard_map/ppermute | solution.py:29
  374.3 10.1 %collective-permute-start.54 = (f32[4,1,16,128]{3,2,1,0:T(8,128)S(1)}, f32[4,1,16,128]{3,2,1,0:T(8,128)S(1)}, u32[]{:S(2)}, u32[]{:S(2)}) collective-permute-start(f32[4,1,16,128]{3,2,1,0:T(8,128)S(1)} %get-tuple-element.93), channel_id=1, source_target_pairs={{1,0},{2,1},{3,2},{4,3},{5,4},{6,5},{7,6},{8,7},{9,8},{10,9},{11,1... | collective-permute-start | bytes 98312 | tf_op jit(solution)/shard_map/ppermute | solution.py:21
  396.5 10.4 %collective-permute-start.57 = (f32[4,1,16,128]{3,2,1,0:T(8,128)S(1)}, f32[4,1,16,128]{3,2,1,0:T(8,128)S(1)}, u32[]{:S(2)}, u32[]{:S(2)}) collective-permute-start(f32[4,1,16,128]{3,2,1,0:T(8,128)S(1)} %get-tuple-element.83), channel_id=1, source_target_pairs={{1,0},{2,1},{3,2},{4,3},{5,4},{6,5},{7,6},{8,7},{9,8},{10,9},{11,1... | collective-permute-start | bytes 98312 | tf_op jit(solution)/shard_map/ppermute | solution.py:21
  398.4 10.0 %collective-permute-start.58 = (f32[4,1,16,128]{3,2,1,0:T(8,128)S(1)}, f32[4,1,16,128]{3,2,1,0:T(8,128)S(1)}, u32[]{:S(2)}, u32[]{:S(2)}) collective-permute-start(f32[4,1,16,128]{3,2,1,0:T(8,128)S(1)} %get-tuple-element.82), channel_id=1, source_target_pairs={{0,1},{1,2},{2,3},{3,4},{4,5},{5,6},{6,7},{7,8},{8,9},{9,10},{10,1... | collective-permute-start | bytes 98312 | tf_op jit(solution)/shard_map/ppermute | solution.py:18
  408.7 12.6 %collective-permute-start.59 = (f32[4,8,16,128]{3,2,1,0:T(8,128)S(1)}, f32[4,8,16,128]{3,2,1,0:T(8,128)S(1)}, u32[]{:S(2)}, u32[]{:S(2)}) collective-permute-start(f32[4,8,16,128]{3,2,1,0:T(8,128)S(1)} %add_add_fusion.5), channel_id=1, source_target_pairs={{0,32},{32,64},{64,96},{96,128},{128,160},{160,192},{192,224},{1,3... | collective-permute-start | bytes 786440 | tf_op jit(solution)/shard_map/ppermute | solution.py:29
  421.7 10.1 %collective-permute-start.60 = (f32[4,1,16,128]{3,2,1,0:T(8,128)S(1)}, f32[4,1,16,128]{3,2,1,0:T(8,128)S(1)}, u32[]{:S(2)}, u32[]{:S(2)}) collective-permute-start(f32[4,1,16,128]{3,2,1,0:T(8,128)S(1)} %get-tuple-element.73), channel_id=1, source_target_pairs={{1,0},{2,1},{3,2},{4,3},{5,4},{6,5},{7,6},{8,7},{9,8},{10,9},{11,1... | collective-permute-start | bytes 98312 | tf_op jit(solution)/shard_map/ppermute | solution.py:21
  443.9 10.4 %collective-permute-start.63 = (f32[4,1,16,128]{3,2,1,0:T(8,128)S(1)}, f32[4,1,16,128]{3,2,1,0:T(8,128)S(1)}, u32[]{:S(2)}, u32[]{:S(2)}) collective-permute-start(f32[4,1,16,128]{3,2,1,0:T(8,128)S(1)} %get-tuple-element.63), channel_id=1, source_target_pairs={{1,0},{2,1},{3,2},{4,3},{5,4},{6,5},{7,6},{8,7},{9,8},{10,9},{11,1... | collective-permute-start | bytes 98312 | tf_op jit(solution)/shard_map/ppermute | solution.py:21
  445.8 10.3 %collective-permute-start.64 = (f32[4,1,16,128]{3,2,1,0:T(8,128)S(1)}, f32[4,1,16,128]{3,2,1,0:T(8,128)S(1)}, u32[]{:S(2)}, u32[]{:S(2)}) collective-permute-start(f32[4,1,16,128]{3,2,1,0:T(8,128)S(1)} %get-tuple-element.62), channel_id=1, source_target_pairs={{0,1},{1,2},{2,3},{3,4},{4,5},{5,6},{6,7},{7,8},{8,9},{9,10},{10,1... | collective-permute-start | bytes 98312 | tf_op jit(solution)/shard_map/ppermute | solution.py:18
  456.4 11.8 %collective-permute-start.65 = (f32[4,8,16,128]{3,2,1,0:T(8,128)S(1)}, f32[4,8,16,128]{3,2,1,0:T(8,128)S(1)}, u32[]{:S(2)}, u32[]{:S(2)}) collective-permute-start(f32[4,8,16,128]{3,2,1,0:T(8,128)S(1)} %add_add_fusion.3), channel_id=1, source_target_pairs={{0,32},{32,64},{64,96},{96,128},{128,160},{160,192},{192,224},{1,3... | collective-permute-start | bytes 786440 | tf_op jit(solution)/shard_map/ppermute | solution.py:29
  468.6 10.1 %collective-permute-start.66 = (f32[4,1,16,128]{3,2,1,0:T(8,128)S(1)}, f32[4,1,16,128]{3,2,1,0:T(8,128)S(1)}, u32[]{:S(2)}, u32[]{:S(2)}) collective-permute-start(f32[4,1,16,128]{3,2,1,0:T(8,128)S(1)} %get-tuple-element.53), channel_id=1, source_target_pairs={{1,0},{2,1},{3,2},{4,3},{5,4},{6,5},{7,6},{8,7},{9,8},{10,9},{11,1... | collective-permute-start | bytes 98312 | tf_op jit(solution)/shard_map/ppermute | solution.py:21
  490.7 10.4 %collective-permute-start.69 = (f32[4,1,16,128]{3,2,1,0:T(8,128)S(1)}, f32[4,1,16,128]{3,2,1,0:T(8,128)S(1)}, u32[]{:S(2)}, u32[]{:S(2)}) collective-permute-start(f32[4,1,16,128]{3,2,1,0:T(8,128)S(1)} %get-tuple-element.43), channel_id=1, source_target_pairs={{1,0},{2,1},{3,2},{4,3},{5,4},{6,5},{7,6},{8,7},{9,8},{10,9},{11,1... | collective-permute-start | bytes 98312 | tf_op jit(solution)/shard_map/ppermute | solution.py:21
  492.7 10.0 %collective-permute-start.70 = (f32[4,1,16,128]{3,2,1,0:T(8,128)S(1)}, f32[4,1,16,128]{3,2,1,0:T(8,128)S(1)}, u32[]{:S(2)}, u32[]{:S(2)}) collective-permute-start(f32[4,1,16,128]{3,2,1,0:T(8,128)S(1)} %get-tuple-element.42), channel_id=1, source_target_pairs={{0,1},{1,2},{2,3},{3,4},{4,5},{5,6},{6,7},{7,8},{8,9},{9,10},{10,1... | collective-permute-start | bytes 98312 | tf_op jit(solution)/shard_map/ppermute | solution.py:18
  513.2 10.4 %collective-permute-start.73 = (f32[4,1,16,128]{3,2,1,0:T(8,128)S(1)}, f32[4,1,16,128]{3,2,1,0:T(8,128)S(1)}, u32[]{:S(2)}, u32[]{:S(2)}) collective-permute-start(f32[4,1,16,128]{3,2,1,0:T(8,128)S(1)} %get-tuple-element.33), channel_id=1, source_target_pairs={{0,1},{1,2},{2,3},{3,4},{4,5},{5,6},{6,7},{7,8},{8,9},{9,10},{10,1... | collective-permute-start | bytes 98312 | tf_op jit(solution)/shard_map/ppermute | solution.py:18
  (29 other events, 255.6 us)
where the time goes:
time: 536 us; the launch traced here: 533 us
  starting transfers between devices  321 us (60%)
  waiting for transfers between devices  186 us (35%)
  other arithmetic  12.5 us (2%)
  local copies, waits for them, and re-layouts  11.6 us (2%)
    ppermute x29, starting transfers between devices, padded_2(): lax.ppermute(lax.slice_in_dim(block, block.shape[dim] - width, None, axis...  229 us
    ppermute x16, waiting for transfers between devices, shifted(): return lax.ppermute(x, axis, pairs)  117 us
    ppermute x29, starting transfers between devices, padded_2(): lax.ppermute(lax.slice_in_dim(block, 0, width, axis=dim), axis, backward)  60.4 us
    ppermute x29, waiting for transfers between devices, padded_2(): lax.ppermute(lax.slice_in_dim(block, 0, width, axis=dim), axis, backward)  38.7 us
    ppermute x16, starting transfers between devices, shifted(): return lax.ppermute(x, axis, pairs)  31 us
    ppermute x29, waiting for transfers between devices, padded_2(): lax.ppermute(lax.slice_in_dim(block, block.shape[dim] - width, None, axis...  30.4 us
  transfers between devices with their start and end apart: 74, of which 41 were waited for; matrix products, arithmetic and copies ran while one was open for 2% of the time, Pallas kernels for 0%

commit v1 on v0

v1 whole, which is shorter than its diff:
```python
import functools
from fractions import Fraction
from math import comb

import jax
import jax.numpy as jnp
import numpy as np
from jax import lax
from jax.experimental import pallas as pl
from jax.experimental.pallas import tpu as pltpu
from jax.sharding import PartitionSpec as P

SWEEPS = 2
SLICES = 8
DT = 0.25
SHIFT = 0.875
MESH = pl.DeviceIdType.MESH


def combine(*terms):
    total = [Fraction(0)] * max(len(p) for _, p in terms)
    for factor, p in terms:
        for k, a in enumerate(p):
            total[k] += Fraction(factor) * a
    return total


def node_polynomials():
    third, small, large = Fraction(1, 3), Fraction(1, 24), Fraction(5, 24)
    half, sixth = Fraction(1, 2), Fraction(1, 6)
    start = [Fraction(1)]

    def image(p):
        return [Fraction(0)] + list(p)

    guesses = [start]
    for _ in range(SLICES - 1):
        guesses.append(combine((1, guesses[-1]), (1, image(guesses[-1]))))
    nodes = [(g, g, g) for g in guesses]
    fine_ends = None
    for sweep in range(SWEEPS):
        starts = guesses if sweep == 0 else [start] + fine_ends[:-1]
        coarse, new_nodes, new_ends = start, [], []
        for n in range(SLICES):
            s = starts[n]
            o0, o1, o2 = (image(u) for u in nodes[n])
            g0 = image(s)
            m = combine((1, s), (half, g0), (-half, o0), (large, o0), (third, o1), (-small, o2))
            g1 = image(m)
            e = combine((1, m), (half, g1), (-half, o1), (-small, o0), (third, o1), (large, o2))
            g2 = image(e)
            c = combine((sixth, g0), (4 * sixth, g1), (sixth, g2), (-1, g0))
            z = combine((1, coarse), (1, image(coarse)), (1, c))
            middle = combine((1, m), (half, coarse), (-half, s), (half, z), (-half, e))
            new_nodes.append((coarse, middle, z))
            new_ends.append(e)
            coarse = z
        nodes, fine_ends = new_nodes, new_ends
    return nodes


def shifted_powers(p, count):
    c = Fraction(SHIFT)
    out = [Fraction(0)] * max(count, len(p))
    for k, a in enumerate(p):
        for j in range(k + 1):
            out[j] += a * comb(k, j) * (-c) ** (k - j)
    assert not any(out[count:])
    return [float(a) for a in out[:count]]


DEGREE = SLICES - 1 + 3 * SWEEPS
W1 = (DEGREE + 1) // 2
W2 = DEGREE - W1
SUMS = 5


def weights():
    nodes = node_polynomials()
    table = []
    for a in range(0, SLICES, 2):
        five = (nodes[a][0], nodes[a][1], nodes[a + 1][0], nodes[a + 1][1], nodes[a + 1][2])
        assert nodes[a][2] == nodes[a + 1][0]
        table.append([shifted_powers(p, DEGREE + 1) for p in five])
    return np.array(table, np.float32)


def kernel(planes, table, initial, velocity, diffusivity, out, power, vel, dif, stencil, sums,
           local_sem, send1, recv1, send2, recv2, send3, recv3):
    count = lax.axis_size("space")
    me = lax.axis_index("space")
    tm = lax.axis_index("tm")
    core = lax.rem(tm, 2)
    pair = lax.div(tm, 2)
    peer = tm + 1 - 2 * core
    has_left = me > 0
    has_right = me < count - 1
    first = 2 * core
    own = pl.ds(W1, planes)

    barrier = pltpu.get_barrier_semaphore()

    @pl.when(has_left)
    def _():
        pl.semaphore_signal(barrier, inc=1, device_id={"space": me - 1}, device_id_type=MESH)

    @pl.when(has_right)
    def _():
        pl.semaphore_signal(barrier, inc=1, device_id={"space": me + 1}, device_id_type=MESH)

    pl.semaphore_signal(barrier, inc=1, device_id={"tm": peer}, device_id_type=MESH)

    loads = [
        pltpu.make_async_copy(initial.at[pl.ds(first, 2)], power.at[0, :, own], local_sem.at[0]),
        pltpu.make_async_copy(velocity, vel.at[:, pl.ds(W1 - 1, planes)], local_sem.at[1]),
        pltpu.make_async_copy(diffusivity, dif.at[pl.ds(W1 - 1, planes)], local_sem.at[2]),
    ]
    for copy in loads:
        copy.start()

    pl.semaphore_wait(barrier, 1 + has_left.astype(jnp.int32) + has_right.astype(jnp.int32))

    def remote(src, dst, send, recv, to):
        return pltpu.make_async_remote_copy(
            src_ref=src, dst_ref=dst, send_sem=send, recv_sem=recv, device_id={"space": to}, device_id_type=MESH
        )

    halo = W1 - 1
    low, high = pl.ds(0, W1), pl.ds(W1 + planes, W1)
    low_c, high_c = pl.ds(0, halo), pl.ds(halo + planes, halo)
    top, bottom = pl.ds(planes - W1, W1), pl.ds(0, W1)
    top_c, bottom_c = pl.ds(planes - halo, halo), pl.ds(0, halo)
    two = pl.ds(first, 2)
    right = jnp.minimum(me + 1, count - 1)
    left = jnp.maximum(me - 1, 0)
    to_right = [
        remote(initial.at[two, top], power.at[0, :, low], send1.at[0, 0], recv1.at[0, 0], right),
        remote(velocity.at[:, top_c], vel.at[:, low_c], send1.at[0, 1], recv1.at[0, 1], right),
        remote(diffusivity.at[top_c], dif.at[low_c], send1.at[0, 2], recv1.at[0, 2], right),
    ]
    to_left = [
        remote(initial.at[two, bottom], power.at[0, :, high], send1.at[1, 0], recv1.at[1, 0], left),
        remote(velocity.at[:, bottom_c], vel.at[:, high_c], send1.at[1, 1], recv1.at[1, 1], left),
        remote(diffusivity.at[bottom_c], dif.at[high_c], send1.at[1, 2], recv1.at[1, 2], left),
    ]

    @pl.when(has_right)
    def _():
        for copy in to_right:
            copy.start()

    @pl.when(has_left)
    def _():
        for copy in to_left:
            copy.start()

    low2, high2 = pl.ds(W1 - W2, W2), pl.ds(W1 + planes, W2)

    @pl.when(jnp.logical_not(has_left))
    def _():
        power[0, :, low] = jnp.zeros((2, W1) + power.shape[3:], jnp.float32)
        power[W1, :, low2] = jnp.zeros((2, W2) + power.shape[3:], jnp.float32)
        vel[:, low_c] = jnp.zeros((3, halo) + power.shape[3:], jnp.float32)
        dif[low_c] = jnp.zeros((halo,) + power.shape[3:], jnp.float32)

    @pl.when(jnp.logical_not(has_right))
    def _():
        power[0, :, high] = jnp.zeros((2, W1) + power.shape[3:], jnp.float32)
        power[W1, :, high2] = jnp.zeros((2, W2) + power.shape[3:], jnp.float32)
        vel[:, high_c] = jnp.zeros((3, halo) + power.shape[3:], jnp.float32)
        dif[high_c] = jnp.zeros((halo,) + power.shape[3:], jnp.float32)

    def derive(lo, hi):
        def one(q, carry):
            d = DT * dif[q]
            for axis in range(3):
                v = (0.5 * DT) * vel[axis, q]
                stencil[2 * axis, q] = d - v
                stencil[2 * axis + 1, q] = d + v
            stencil[6, q] = SHIFT - 6.0 * d
            return carry

        lax.fori_loop(lo, hi, one, 0, unroll=2)

    def advance(k, lo, hi):
        def one(q, carry):
            c = [stencil[j, q - 1] for j in range(7)]
            for t in range(2):
                u = power[k - 1, t, q]
                x = c[0] * power[k - 1, t, q + 1] + c[1] * power[k - 1, t, q - 1]
                y = c[2] * pltpu.roll(u, u.shape[0] - 1, 0) + c[3] * pltpu.roll(u, 1, 0)
                z = c[4] * pltpu.roll(u, u.shape[1] - 1, 1) + c[5] * pltpu.roll(u, 1, 1)
                power[k, t, q] = (x + y) + (z + c[6] * u)
            return carry

        lax.fori_loop(lo, hi, one, 0, unroll=2)

    for copy in loads:
        copy.wait()
    derive(halo, halo + planes)

    @pl.when(has_right)
    def _():
        for copy in to_right:
            copy.wait_send()
        for copy in to_left:
            copy.wait_recv()

    @pl.when(has_left)
    def _():
        for copy in to_left:
            copy.wait_send()
        for copy in to_right:
            copy.wait_recv()

    derive(0, halo)
    derive(halo + planes, 2 * halo + planes)
    for k in range(1, W1 + 1):
        advance(k, k, 2 * W1 + planes - k)

    again_right = remote(
        power.at[W1, :, pl.ds(W1 + planes - W2, W2)], power.at[W1, :, low2], send2.at[0], recv2.at[0], right
    )
    again_left = remote(power.at[W1, :, pl.ds(W1, W2)], power.at[W1, :, high2], send2.at[1], recv2.at[1], left)

    @pl.when(has_right)
    def _():
        again_right.start()

    @pl.when(has_left)
    def _():
        again_left.start()

    def accumulate(lo, hi):
        def one(q, carry):
            for t in range(2):
                v = [power[k, t, q + W1] for k in range(lo, hi)]
                for j in range(SUMS):
                    total = sums[j, t, q] if lo else None
                    for k in range(lo, hi):
                        term = table[(pair * SUMS + j) * (DEGREE + 1) + k] * v[k - lo]
                        total = term if total is None else total + term
                    sums[j, t, q] = total
            return carry

        lax.fori_loop(0, planes, one, 0)

    accumulate(0, W1 + 1)

    @pl.when(has_right)
    def _():
        again_right.wait_send()
        again_left.wait_recv()

    @pl.when(has_left)
    def _():
        again_left.wait_send()
        again_right.wait_recv()

    for k in range(W1 + 1, DEGREE + 1):
        advance(k, 1 + k - W1, 2 * W1 + planes - 1 - (k - W1))
    accumulate(W1 + 1, DEGREE + 1)

    across = pltpu.make_async_remote_copy(
        src_ref=sums.at[pl.ds(2 - 2 * core, 3)],
        dst_ref=out.at[:, two],
        send_sem=send3,
        recv_sem=recv3,
        device_id={"tm": peer},
        device_id_type=MESH,
    )
    across.start()
    keep = pltpu.make_async_copy(sums.at[pl.ds(2 * core, 3)], out.at[:, two], local_sem.at[3])
    keep.start()
    keep.wait()
    across.wait()


def body(initial, velocity, diffusivity):
    planes, rows, lanes = diffusivity.shape
    table = jnp.asarray(weights().reshape(-1))
    anywhere = pl.BlockSpec(memory_space=pl.ANY)
    halo = W1 - 1
    nodes = pl.pallas_call(
        functools.partial(kernel, planes),
        out_shape=jax.ShapeDtypeStruct((3,) + initial.shape, jnp.float32),
        in_specs=[pl.BlockSpec(memory_space=pltpu.SMEM), anywhere, anywhere, anywhere],
        out_specs=anywhere,
        scratch_shapes=[
            pltpu.VMEM((DEGREE + 1, 2, planes + 2 * W1, rows, lanes), jnp.float32),
            pltpu.VMEM((3, planes + 2 * halo, rows, lanes), jnp.float32),
            pltpu.VMEM((planes + 2 * halo, rows, lanes), jnp.float32),
            pltpu.VMEM((7, planes + 2 * halo, rows, lanes), jnp.float32),
            pltpu.VMEM((SUMS, 2, planes, rows, lanes), jnp.float32),
            pltpu.SemaphoreType.DMA((4,)),
            pltpu.SemaphoreType.DMA((2, 3)),
            pltpu.SemaphoreType.DMA((2, 3)),
            pltpu.SemaphoreType.DMA((2,)),
            pltpu.SemaphoreType.DMA((2,)),
            pltpu.SemaphoreType.DMA,
            pltpu.SemaphoreType.DMA,
        ],
        compiler_params=pltpu.CompilerParams(collective_id=0, has_side_effects=True, vmem_limit_bytes=24 * 2**20),
        name="powers",
    )(table, initial, velocity, diffusivity)
    return nodes[None]


def solution(mesh):
    return jax.shard_map(
        body,
        mesh=mesh,
        in_specs=(
            P(None, "space", None, None),
            P(None, "space", None, None),
            P("space", None, None),
        ),
        out_specs=P("tm", None, None, "space", None, None),
        check_vma=False,
    )
```

time: 536 us -> 37.8 us (0.07)
  the two profiles are of different devices: /device:TPU:158 before, /device:TPU:161 now
where the time goes in v1:
time: 37.8 us; the launch traced here: 37.6 us
  Pallas kernels  33.3 us (88%)
  local copies, waits for them, and re-layouts  4.28 us (11%)
    pallas_call x1, Pallas kernels, body(): pl.pallas_call(functools.partial(kernel, planes), out_shape=jax.ShapeDtyp...  33.3 us
    unnamed x9, local copies, waits for them, and re-layouts  4.28 us

profile of v1, /device:TPU:161, one launch (start us, length us, event | category | flops | bytes accessed | tf_op | source)
XLA Modules:
  0.0 37.6 jit_solution(10547962485549779432)
XLA Ops:
  0.0 0.0 copy-start
  0.0 0.9 %copy-done = f32[4,8,16,128]{3,2,1,0:T(8,128)S(1)} copy-done((f32[4,8,16,128]{3,2,1,0:T(8,128)S(1)}, f32[4,8,16,128]{3,2,1,0:T(8,128)}, u32[]{:S(2)}) %copy-start) | copy-done | bytes 262168
  1.0 0.0 copy-start.1
  1.0 0.9 %copy-done.1 = f32[3,8,16,128]{3,2,1,0:T(8,128)S(1)} copy-done((f32[3,8,16,128]{3,2,1,0:T(8,128)S(1)}, f32[3,8,16,128]{3,2,1,0:T(8,128)}, u32[]{:S(2)}) %copy-start.1) | copy-done | bytes 196632
  1.9 0.0 copy-start.2
  1.9 0.8 %copy-done.2 = f32[8,16,128]{2,1,0:T(8,128)S(1)} copy-done((f32[8,16,128]{2,1,0:T(8,128)S(1)}, f32[8,16,128]{2,1,0:T(8,128)}, u32[]{:S(2)}) %copy-start.2) | copy-done | bytes 65560
  2.7 0.0 copy-start.3
  2.7 0.7 %copy-done.3 = f32[280]{0:T(512)S(1)} copy-done((f32[280]{0:T(512)S(1)}, f32[280]{0:T(512)}, u32[]{:S(2)}) %copy-start.3) | copy-done | bytes 1144
  3.4 33.3 %powers.1 = f32[3,4,8,16,128]{4,3,2,1,0:T(8,128)S(1)} custom-call(f32[280]{0:T(512)S(1)} %copy-done.3, f32[4,8,16,128]{3,2,1,0:T(8,128)S(1)} %copy-done, f32[3,8,16,128]{3,2,1,0:T(8,128)S(1)} %copy-done.1, f32[8,16,128]{2,1,0:T(8,128)S(1)} %copy-done.2), custom_call_target="tpu_custom_call" | custom-call | tf_op jit(solution)/shard_map/powers/pallas_call | solution.py:284
  36.7 0.9 %copy.6 = f32[1,3,4,8,16,128]{5,4,3,2,1,0:T(8,128)} copy(f32[1,3,4,8,16,128]{5,4,3,2,1,0:T(8,128)S(1)} %bitcast.1) | data formatting | bytes 1572864
Async XLA Ops:
  0.0 0.9 %copy-start = (f32[4,8,16,128]{3,2,1,0:T(8,128)S(1)}, f32[4,8,16,128]{3,2,1,0:T(8,128)}, u32[]{:S(2)}) copy-start(f32[4,8,16,128]{3,2,1,0:T(8,128)} %initial.1) | copy-start | bytes 786436
  1.0 0.9 %copy-start.1 = (f32[3,8,16,128]{3,2,1,0:T(8,128)S(1)}, f32[3,8,16,128]{3,2,1,0:T(8,128)}, u32[]{:S(2)}) copy-start(f32[3,8,16,128]{3,2,1,0:T(8,128)} %velocity.1) | copy-start | bytes 589828
  1.9 0.8 %copy-start.2 = (f32[8,16,128]{2,1,0:T(8,128)S(1)}, f32[8,16,128]{2,1,0:T(8,128)}, u32[]{:S(2)}) copy-start(f32[8,16,128]{2,1,0:T(8,128)} %diffusivity.1) | copy-start | bytes 196612
  2.7 0.7 %copy-start.3 = (f32[280]{0:T(512)S(1)}, f32[280]{0:T(512)}, u32[]{:S(2)}) copy-start(f32[280]{0:T(512)} %constant.2.clone.table) | copy-start | bytes 3364

commit v2 on v1

--- a/solution.py
+++ b/solution.py
@@ -193,7 +193,7 @@
                 power[k, t, q] = (x + y) + (z + c[6] * u)
             return carry
 
-        lax.fori_loop(lo, hi, one, 0, unroll=2)
+        lax.fori_loop(lo, hi, one, 0, unroll=True)
 
     for copy in loads:
         copy.wait()
@@ -302,7 +302,7 @@
         ],
         compiler_params=pltpu.CompilerParams(collective_id=0, has_side_effects=True, vmem_limit_bytes=24 * 2**20),
         name="powers",
-    )(table, initial, velocity, diffusivity)
+    )(table, *[pltpu.with_memory_space_constraint(a, pltpu.HBM) for a in (initial, velocity, diffusivity)])
     return nodes[None]
 
 

time: 37.8 us -> 28.5 us (0.75)
  Pallas kernels: 33.3 us -> 26.8 us
  local copies, waits for them, and re-layouts: 4.28 us -> 1.56 us
    pallas_call x1, Pallas kernels: 33.3 us -> 26.8 us  [body(): pl.pallas_call(functools.partial(kernel, planes), out_shape=jax.ShapeDtyp...]
    unnamed x9 -> x3, local copies, waits for them, and re-layouts: 4.28 us -> 1.56 us
where the time goes in v2:
time: 28.5 us; the launch traced here: 28.4 us
  Pallas kernels  26.8 us (94%)
  local copies, waits for them, and re-layouts  1.56 us (5%)
    pallas_call x1, Pallas kernels, body(): pl.pallas_call(functools.partial(kernel, planes), out_shape=jax.ShapeDtyp...  26.8 us
    unnamed x3, local copies, waits for them, and re-layouts  1.56 us

profile of v2, /device:TPU:161, one launch (start us, length us, event | category | flops | bytes accessed | tf_op | source)
XLA Modules:
  0.0 28.4 jit_solution(14086236688448183201)
XLA Ops:
  0.0 0.0 copy-start
  0.0 0.7 %copy-done = f32[280]{0:T(512)S(1)} copy-done((f32[280]{0:T(512)S(1)}, f32[280]{0:T(512)}, u32[]{:S(2)}) %copy-start) | copy-done | bytes 1144
  0.7 26.8 %powers.1 = f32[3,4,8,16,128]{4,3,2,1,0:T(8,128)S(1)} custom-call(f32[280]{0:T(512)S(1)} %copy-done, f32[4,8,16,128]{3,2,1,0:T(8,128)} %initial.1, f32[3,8,16,128]{3,2,1,0:T(8,128)} %velocity.1, f32[8,16,128]{2,1,0:T(8,128)} %diffusivity.1), custom_call_target="tpu_custom_call" | custom-call | tf_op jit(solution)/shard_map/powers/pallas_call | solution.py:284
  27.5 0.9 %copy.6 = f32[1,3,4,8,16,128]{5,4,3,2,1,0:T(8,128)} copy(f32[1,3,4,8,16,128]{5,4,3,2,1,0:T(8,128)S(1)} %bitcast.1) | data formatting | bytes 1572864
Async XLA Ops:
  0.0 0.7 %copy-start = (f32[280]{0:T(512)S(1)}, f32[280]{0:T(512)}, u32[]{:S(2)}) copy-start(f32[280]{0:T(512)} %constant.2.clone.table) | copy-start | bytes 3364

commit v3 on v2

v3 whole, which is shorter than its diff:
```python
import functools
from fractions import Fraction
from math import comb

import jax
import jax.numpy as jnp
import numpy as np
from jax import lax
from jax.experimental import pallas as pl
from jax.experimental.pallas import tpu as pltpu
from jax.sharding import PartitionSpec as P

SWEEPS = 2
SLICES = 8
DT = 0.25
SHIFT = 0.875
MESH = pl.DeviceIdType.MESH


def combine(*terms):
    total = [Fraction(0)] * max(len(p) for _, p in terms)
    for factor, p in terms:
        for k, a in enumerate(p):
            total[k] += Fraction(factor) * a
    return total


def node_polynomials():
    third, small, large = Fraction(1, 3), Fraction(1, 24), Fraction(5, 24)
    half, sixth = Fraction(1, 2), Fraction(1, 6)
    start = [Fraction(1)]

    def image(p):
        return [Fraction(0)] + list(p)

    guesses = [start]
    for _ in range(SLICES - 1):
        guesses.append(combine((1, guesses[-1]), (1, image(guesses[-1]))))
    nodes = [(g, g, g) for g in guesses]
    fine_ends = None
    for sweep in range(SWEEPS):
        starts = guesses if sweep == 0 else [start] + fine_ends[:-1]
        coarse, new_nodes, new_ends = start, [], []
        for n in range(SLICES):
            s = starts[n]
            o0, o1, o2 = (image(u) for u in nodes[n])
            g0 = image(s)
            m = combine((1, s), (half, g0), (-half, o0), (large, o0), (third, o1), (-small, o2))
            g1 = image(m)
            e = combine((1, m), (half, g1), (-half, o1), (-small, o0), (third, o1), (large, o2))
            g2 = image(e)
            c = combine((sixth, g0), (4 * sixth, g1), (sixth, g2), (-1, g0))
            z = combine((1, coarse), (1, image(coarse)), (1, c))
            middle = combine((1, m), (half, coarse), (-half, s), (half, z), (-half, e))
            new_nodes.append((coarse, middle, z))
            new_ends.append(e)
            coarse = z
        nodes, fine_ends = new_nodes, new_ends
    return nodes


def shifted_powers(p, count):
    c = Fraction(SHIFT)
    out = [Fraction(0)] * max(count, len(p))
    for k, a in enumerate(p):
        for j in range(k + 1):
            out[j] += a * comb(k, j) * (-c) ** (k - j)
    assert not any(out[count:])
    return [float(a) for a in out[:count]]


DEGREE = SLICES - 1 + 3 * SWEEPS
W1 = 5
W2 = DEGREE - W1
EDGE = max(W1, W2)
HALO = EDGE - 1
NEAR = W1 - 1
FAR = HALO - NEAR
SUMS = 5
LANES = 128


def weights():
    nodes = node_polynomials()
    table = np.zeros((SLICES, LANES), np.float32)
    for n in range(SLICES):
        a = n - n % 2
        assert nodes[a][2] == nodes[a + 1][0]
        own, other = (nodes[a][:2], nodes[a + 1][1:]) if n == a else (nodes[a + 1][1:], nodes[a][:2])
        row = [shifted_powers(p, DEGREE + 1) for p in (nodes[a][2], *own, *other)]
        table[n, : SUMS * (DEGREE + 1)] = np.reshape(row, -1)
    return table


def kernel(planes, weight_rows, initial, velocity, diffusivity, out, power, raw, stencil, sums, across, weight,
           local_sem, send, recv, pass_send, pass_recv, cross_send, cross_recv):
    count = lax.axis_size("space")
    me = lax.axis_index("space")
    tm = lax.axis_index("tm")
    core = lax.rem(tm, 2)
    peer = tm + 1 - 2 * core
    has_left = me > 0
    has_right = me < count - 1
    left = jnp.maximum(me - 1, 0)
    right = jnp.minimum(me + 1, count - 1)
    first = 2 * core
    two = pl.ds(first, 2)
    tile = power.shape[3:]

    barrier = pltpu.get_barrier_semaphore()

    @pl.when(has_left)
    def _():
        pl.semaphore_signal(barrier, inc=1, device_id={"space": me - 1}, device_id_type=MESH)

    @pl.when(has_right)
    def _():
        pl.semaphore_signal(barrier, inc=1, device_id={"space": me + 1}, device_id_type=MESH)

    pl.semaphore_signal(barrier, inc=1, device_id={"tm": peer}, device_id_type=MESH)

    loads = [
        pltpu.make_async_copy(velocity, raw.at[pl.ds(0, 3), pl.ds(HALO, planes)], local_sem.at[0]),
        pltpu.make_async_copy(diffusivity, raw.at[3, pl.ds(HALO, planes)], local_sem.at[1]),
        pltpu.make_async_copy(initial.at[two], power.at[0, :, pl.ds(EDGE, planes)], local_sem.at[2]),
        pltpu.make_async_copy(weight_rows, weight, local_sem.at[3]),
    ]
    for copy in loads:
        copy.start()

    def clear(edge, halo):
        power[0, :, pl.ds(edge, EDGE)] = jnp.zeros((2, EDGE) + tile, jnp.float32)
        power[W1, :, pl.ds(edge, EDGE)] = jnp.zeros((2, EDGE) + tile, jnp.float32)
        raw[:, pl.ds(halo, HALO)] = jnp.zeros((4, HALO) + tile, jnp.float32)

    @pl.when(jnp.logical_not(has_left))
    def _():
        clear(0, 0)

    @pl.when(jnp.logical_not(has_right))
    def _():
        clear(EDGE + planes, HALO + planes)

    def remote(side, item, src, dst):
        return pltpu.make_async_remote_copy(
            src_ref=src,
            dst_ref=dst,
            send_sem=send.at[side, item],
            recv_sem=recv.at[side, item],
            device_id={"space": left if side else right},
            device_id_type=MESH,
        )

    def field_halo(side, item, level, t, width):
        src = EDGE if side else EDGE + planes - width
        dst = EDGE + planes if side else EDGE - width
        return remote(side, item, power.at[level, t, pl.ds(src, width)], power.at[level, t, pl.ds(dst, width)])

    def near_at(side):
        return pl.ds(HALO + planes if side else HALO - NEAR, NEAR)

    def far_at(side):
        return pl.ds(HALO + planes + NEAR if side else 0, FAR)

    def passed(item, side, at):
        ref = raw.at[two, at]
        return pltpu.make_async_remote_copy(
            src_ref=ref,
            dst_ref=ref,
            send_sem=pass_send.at[item, side],
            recv_sem=pass_recv.at[item, side],
            device_id={"tm": peer},
            device_id_type=MESH,
        )

    near, far, first_round, second_round, near_pass, far_pass = [], [], [[], []], [[], []], [], []
    for side in range(2):
        src = HALO if side else HALO + planes - NEAR
        near.append(remote(side, 0, raw.at[two, pl.ds(src, NEAR)], raw.at[two, near_at(side)]))
        src = HALO + NEAR if side else HALO + planes - HALO
        far.append(remote(side, 1, raw.at[two, pl.ds(src, FAR)], raw.at[two, far_at(side)]))
        near_pass.append(passed(0, side, near_at(side)))
        far_pass.append(passed(1, side, far_at(side)))
        for t in range(2):
            first_round[t].append(field_halo(side, 2 + t, 0, t, W1))
            second_round[t].append(field_halo(side, 4 + t, W1, t, W2))

    def start(*pairs):
        @pl.when(has_right)
        def _():
            for pair in pairs:
                pair[0].start()

        @pl.when(has_left)
        def _():
            for pair in pairs:
                pair[1].start()

    def arrived(pair, then=None):
        @pl.when(has_left)
        def _():
            pair[0].wait_recv()
            if then:
                then[0].start()

        @pl.when(has_right)
        def _():
            pair[1].wait_recv()
            if then:
                then[1].start()

    def derive(lo, hi):
        for q in range(lo, hi):
            d = DT * raw[3, q]
            for axis in range(3):
                v = (0.5 * DT) * raw[axis, q]
                stencil[2 * axis, q] = d - v
                stencil[2 * axis + 1, q] = d + v
            stencil[6, q] = SHIFT - 6.0 * d

    def advance(t, k, lo, hi):
        for q in range(lo, hi):
            c = [stencil[j, q - 1] for j in range(7)]
            u = power[k - 1, t, q]
            x = c[0] * power[k - 1, t, q + 1] + c[1] * power[k - 1, t, q - 1]
            y = c[2] * pltpu.roll(u, u.shape[0] - 1, 0) + c[3] * pltpu.roll(u, 1, 0)
            z = c[4] * pltpu.roll(u, u.shape[1] - 1, 1) + c[5] * pltpu.roll(u, 1, 1)
            power[k, t, q] = (x + y) + (z + c[6] * u)

    def accumulate(t, p, lo, hi, before):
        v = [power[k, t, p + EDGE] for k in range(lo, hi)]
        totals = []
        for j in range(SUMS):
            total = before[j] if before else None
            for k in range(lo, hi):
                term = weight[tm, j * (DEGREE + 1) + k] * v[k - lo]
                total = term if total is None else total + term
            totals.append(total)
        return totals

    for copy in loads:
        copy.wait()
    derive(HALO, HALO + planes)

    pl.semaphore_wait(barrier, 1 + has_left.astype(jnp.int32) + has_right.astype(jnp.int32))
    start(near, first_round[0], first_round[1], far)

    arrived(near, near_pass)
    arrived(near_pass)
    derive(HALO - NEAR, HALO)
    derive(HALO + planes, HALO + planes + NEAR)
    for t in range(2):
        arrived(first_round[t])
        for k in range(1, W1 + 1):
            advance(t, k, EDGE - W1 + k, EDGE + planes + W1 - k)
        start(second_round[t])

    arrived(far, far_pass)
    for t in range(2):
        for p in range(planes):
            for j, total in enumerate(accumulate(t, p, 0, W1 + 1, None)):
                sums[j, t, p] = total
    arrived(far_pass)
    derive(0, FAR)
    derive(HALO + planes + NEAR, 2 * HALO + planes)

    crossings = []
    for t in range(2):
        arrived(second_round[t])
        for j in range(1, W2 + 1):
            advance(t, W1 + j, EDGE - W2 + j, EDGE + planes + W2 - j)
        for p in range(planes):
            totals = accumulate(t, p, W1 + 1, DEGREE + 1, [sums[j, t, p] for j in range(SUMS)])
            out[2 - 2 * core, first + t, p] = totals[0]
            out[core, first + t, p] = totals[1]
            out[core + 1, first + t, p] = totals[2]
            across[t, 2 * core, p] = totals[0]
            across[t, 1 - core, p] = totals[3]
            across[t, 2 - core, p] = totals[4]
        crossings.append(
            pltpu.make_async_remote_copy(
                src_ref=across.at[t],
                dst_ref=out.at[:, first + t],
                send_sem=cross_send.at[t],
                recv_sem=cross_recv.at[t],
                device_id={"tm": peer},
                device_id_type=MESH,
            )
        )
        crossings[t].start()

    everything = [near, far, *first_round, *second_round]

    @pl.when(has_right)
    def _():
        for pair in everything:
            pair[0].wait_send()
        near_pass[1].wait_send()
        far_pass[1].wait_send()

    @pl.when(has_left)
    def _():
        for pair in everything:
            pair[1].wait_send()
        near_pass[0].wait_send()
        far_pass[0].wait_send()

    for copy in crossings:
        copy.wait()


def body(initial, velocity, diffusivity):
    planes, rows, lanes = diffusivity.shape
    operands = (jnp.asarray(weights()), initial, velocity, diffusivity)
    nodes = pl.pallas_call(
        functools.partial(kernel, planes),
        out_shape=jax.ShapeDtypeStruct((3,) + initial.shape, jnp.float32),
        in_specs=[pl.BlockSpec(memory_space=pl.ANY)] * 4,
        out_specs=pl.BlockSpec(memory_space=pltpu.VMEM),
        scratch_shapes=[
            pltpu.VMEM((DEGREE + 1, 2, planes + 2 * EDGE, rows, lanes), jnp.float32),
            pltpu.VMEM((4, planes + 2 * HALO, rows, lanes), jnp.float32),
            pltpu.VMEM((7, planes + 2 * HALO, rows, lanes), jnp.float32),
            pltpu.VMEM((SUMS, 2, planes, rows, lanes), jnp.float32),
            pltpu.VMEM((2, 3, planes, rows, lanes), jnp.float32),
            pltpu.SMEM((SLICES, LANES), jnp.float32),
            pltpu.SemaphoreType.DMA((4,)),
            pltpu.SemaphoreType.DMA((2, 6)),
            pltpu.SemaphoreType.DMA((2, 6)),
            pltpu.SemaphoreType.DMA((2, 2)),
            pltpu.SemaphoreType.DMA((2, 2)),
            pltpu.SemaphoreType.DMA((2,)),
            pltpu.SemaphoreType.DMA((2,)),
        ],
        compiler_params=pltpu.CompilerParams(collective_id=0, has_side_effects=True, vmem_limit_bytes=24 * 2**20),
        name="powers",
    )(*[pltpu.with_memory_space_constraint(a, pltpu.HBM) for a in operands])
    return nodes[None]


def solution(mesh):
    return jax.shard_map(
        body,
        mesh=mesh,
        in_specs=(
            P(None, "space", None, None),
            P(None, "space", None, None),
            P("space", None, None),
        ),
        out_specs=P("tm", None, None, "space", None, None),
        check_vma=False,
    )
```

time: 28.5 us -> 24 us (0.84)
  Pallas kernels: 26.8 us -> 23 us
  local copies, waits for them, and re-layouts: 1.56 us -> 0.88 us
    pallas_call x1, Pallas kernels: 26.8 us -> 23 us  [body(): pl.pallas_call(functools.partial(kernel, planes), out_shape=jax.ShapeDtyp...]
    unnamed x3 -> x1, local copies, waits for them, and re-layouts: 1.56 us -> 0.88 us
where the time goes in v3:
time: 24 us; the launch traced here: 23.9 us
  Pallas kernels  23 us (96%)
  local copies, waits for them, and re-layouts  0.88 us (4%)
    pallas_call x1, Pallas kernels, body(): pl.pallas_call(functools.partial(kernel, planes), out_shape=jax.ShapeDtyp...  23 us
    unnamed x1, local copies, waits for them, and re-layouts  0.88 us

profile of v3, /device:TPU:161, one launch (start us, length us, event | category | flops | bytes accessed | tf_op | source)
XLA Modules:
  0.0 23.9 jit_solution(16631118868665655202)
XLA Ops:
  0.0 23.0 %powers.1 = f32[3,4,8,16,128]{4,3,2,1,0:T(8,128)S(1)} custom-call(f32[8,128]{1,0:T(8,128)} %constant.2.clone.weight_rows, f32[4,8,16,128]{3,2,1,0:T(8,128)} %initial.1, f32[3,8,16,128]{3,2,1,0:T(8,128)} %velocity.1, f32[8,16,128]{2,1,0:T(8,128)} %diffusivity.1), custom_call_target="tpu_custom_call" | custom-call | tf_op jit(solution)/shard_map/powers/pallas_call | solution.py:315
  23.0 0.9 %copy.6 = f32[1,3,4,8,16,128]{5,4,3,2,1,0:T(8,128)} copy(f32[1,3,4,8,16,128]{5,4,3,2,1,0:T(8,128)S(1)} %bitcast.1) | data formatting | bytes 1572864

commit v4 on v3

--- a/solution.py
+++ b/solution.py
@@ -70,13 +70,13 @@
 
 
 DEGREE = SLICES - 1 + 3 * SWEEPS
-W1 = 5
+W1 = 7
 W2 = DEGREE - W1
-EDGE = max(W1, W2)
+EDGE = W1 + W2
 HALO = EDGE - 1
 NEAR = W1 - 1
-FAR = HALO - NEAR
 SUMS = 5
+GROUP = 16
 LANES = 128
 
 
@@ -103,6 +103,10 @@
     has_right = me < count - 1
     left = jnp.maximum(me - 1, 0)
     right = jnp.minimum(me + 1, count - 1)
+    slow_left = jnp.logical_and(has_left, lax.rem(me, GROUP) == 0)
+    slow_right = jnp.logical_and(has_right, lax.rem(me + 1, GROUP) == 0)
+    fast_left = jnp.logical_and(has_left, jnp.logical_not(slow_left))
+    fast_right = jnp.logical_and(has_right, jnp.logical_not(slow_right))
     first = 2 * core
     two = pl.ds(first, 2)
     tile = power.shape[3:]
@@ -128,18 +132,18 @@
     for copy in loads:
         copy.start()
 
-    def clear(edge, halo):
-        power[0, :, pl.ds(edge, EDGE)] = jnp.zeros((2, EDGE) + tile, jnp.float32)
-        power[W1, :, pl.ds(edge, EDGE)] = jnp.zeros((2, EDGE) + tile, jnp.float32)
-        raw[:, pl.ds(halo, HALO)] = jnp.zeros((4, HALO) + tile, jnp.float32)
+    def clear(first_at, second_at, near_at):
+        power[0, :, pl.ds(first_at, W1)] = jnp.zeros((2, W1) + tile, jnp.float32)
+        power[W1, :, pl.ds(second_at, W2)] = jnp.zeros((2, W2) + tile, jnp.float32)
+        raw[:, pl.ds(near_at, NEAR)] = jnp.zeros((4, NEAR) + tile, jnp.float32)
 
     @pl.when(jnp.logical_not(has_left))
     def _():
-        clear(0, 0)
+        clear(EDGE - W1, EDGE - W2, HALO - NEAR)
 
     @pl.when(jnp.logical_not(has_right))
     def _():
-        clear(EDGE + planes, HALO + planes)
+        clear(EDGE + planes, EDGE + planes, HALO + planes)
 
     def remote(side, item, src, dst):
         return pltpu.make_async_remote_copy(
@@ -156,14 +160,8 @@
         dst = EDGE + planes if side else EDGE - width
         return remote(side, item, power.at[level, t, pl.ds(src, width)], power.at[level, t, pl.ds(dst, width)])
 
-    def near_at(side):
-        return pl.ds(HALO + planes if side else HALO - NEAR, NEAR)
-
-    def far_at(side):
-        return pl.ds(HALO + planes + NEAR if side else 0, FAR)
-
-    def passed(item, side, at):
-        ref = raw.at[two, at]
+    def passed(item, side, at, width):
+        ref = raw.at[two, pl.ds(at, width)]
         return pltpu.make_async_remote_copy(
             src_ref=ref,
             dst_ref=ref,
@@ -173,44 +171,46 @@
             device_id_type=MESH,
         )
 
-    near, far, first_round, second_round, near_pass, far_pass = [], [], [[], []], [[], []], [], []
+    near, first_round, second_round, near_pass = [], [[], []], [[], []], []
+    deep, deep_fields, deep_pass = [], [[], []], []
     for side in range(2):
         src = HALO if side else HALO + planes - NEAR
-        near.append(remote(side, 0, raw.at[two, pl.ds(src, NEAR)], raw.at[two, near_at(side)]))
-        src = HALO + NEAR if side else HALO + planes - HALO
-        far.append(remote(side, 1, raw.at[two, pl.ds(src, FAR)], raw.at[two, far_at(side)]))
-        near_pass.append(passed(0, side, near_at(side)))
-        far_pass.append(passed(1, side, far_at(side)))
+        dst = HALO + planes if side else HALO - NEAR
+        near.append(remote(side, 0, raw.at[two, pl.ds(src, NEAR)], raw.at[two, pl.ds(dst, NEAR)]))
+        near_pass.append(passed(0, side, dst, NEAR))
         for t in range(2):
             first_round[t].append(field_halo(side, 2 + t, 0, t, W1))
             second_round[t].append(field_halo(side, 4 + t, W1, t, W2))
-
-    def start(*pairs):
-        @pl.when(has_right)
-        def _():
-            for pair in pairs:
-                pair[0].start()
-
-        @pl.when(has_left)
-        def _():
-            for pair in pairs:
-                pair[1].start()
-
-    def arrived(pair, then=None):
-        @pl.when(has_left)
-        def _():
-            pair[0].wait_recv()
-            if then:
-                then[0].start()
-
-        @pl.when(has_right)
-        def _():
-            pair[1].wait_recv()
-            if then:
-                then[1].start()
-
-    def derive(lo, hi):
-        for q in range(lo, hi):
+        src = HALO + NEAR if side else HALO + planes - NEAR - W2
+        dst = src + planes if side else src - planes
+        deep.append(remote(side, 1, raw.at[two, pl.ds(src, W2)], raw.at[two, pl.ds(dst, W2)]))
+        deep_pass.append(passed(1, side, dst, W2))
+        src = EDGE + W1 if side else EDGE + planes - W1 - W2
+        dst = src + planes if side else src - planes
+        for t in range(2):
+            deep_fields[t].append(
+                remote(side, 6 + t, power.at[0, t, pl.ds(src, W2)], power.at[0, t, pl.ds(dst, W2)])
+            )
+
+    def start(to_right, to_left, *pairs):
+        for side, there in ((0, to_right), (1, to_left)):
+
+            @pl.when(there)
+            def _():
+                for pair in pairs:
+                    pair[side].start()
+
+    def arrived(from_left, from_right, pair, then=None):
+        for side, there in ((0, from_left), (1, from_right)):
+
+            @pl.when(there)
+            def _():
+                pair[side].wait_recv()
+                if then:
+                    then[side].start()
+
+    def derive(lo, width):
+        for q in [lo + i for i in range(width)]:
             d = DT * raw[3, q]
             for axis in range(3):
                 v = (0.5 * DT) * raw[axis, q]
@@ -218,8 +218,8 @@
                 stencil[2 * axis + 1, q] = d + v
             stencil[6, q] = SHIFT - 6.0 * d
 
-    def advance(t, k, lo, hi):
-        for q in range(lo, hi):
+    def advance(t, k, lo, width):
+        for q in [lo + i for i in range(width)]:
             c = [stencil[j, q - 1] for j in range(7)]
             u = power[k - 1, t, q]
             x = c[0] * power[k - 1, t, q + 1] + c[1] * power[k - 1, t, q - 1]
@@ -240,35 +240,55 @@
 
     for copy in loads:
         copy.wait()
-    derive(HALO, HALO + planes)
+    derive(HALO, planes)
 
     pl.semaphore_wait(barrier, 1 + has_left.astype(jnp.int32) + has_right.astype(jnp.int32))
-    start(near, first_round[0], first_round[1], far)
-
-    arrived(near, near_pass)
-    arrived(near_pass)
-    derive(HALO - NEAR, HALO)
-    derive(HALO + planes, HALO + planes + NEAR)
+    start(has_right, has_left, near, *first_round)
+
+    for side, there in ((0, slow_right), (1, slow_left)):
+
+        @pl.when(there)
+        def _():
+            near[side].wait_recv()
+            deep[side].start()
+            near_pass[side].start()
+            for t in range(2):
+                first_round[t][side].wait_recv()
+                deep_fields[t][side].start()
+
+    from_left = jnp.logical_and(has_left, jnp.logical_not(slow_right))
+    from_right = jnp.logical_and(has_right, jnp.logical_not(slow_left))
+    arrived(from_left, from_right, near, near_pass)
+    arrived(has_left, has_right, near_pass)
+    derive(HALO - NEAR, NEAR)
+    derive(HALO + planes, NEAR)
     for t in range(2):
-        arrived(first_round[t])
+        arrived(from_left, from_right, first_round[t])
         for k in range(1, W1 + 1):
-            advance(t, k, EDGE - W1 + k, EDGE + planes + W1 - k)
-        start(second_round[t])
-
-    arrived(far, far_pass)
+            advance(t, k, EDGE - W1 + k, planes + 2 * (W1 - k))
+        start(fast_right, fast_left, second_round[t])
+
     for t in range(2):
         for p in range(planes):
             for j, total in enumerate(accumulate(t, p, 0, W1 + 1, None)):
                 sums[j, t, p] = total
-    arrived(far_pass)
-    derive(0, FAR)
-    derive(HALO + planes + NEAR, 2 * HALO + planes)
+
+    arrived(slow_left, slow_right, deep, deep_pass)
+
+    @pl.when(jnp.logical_or(slow_left, slow_right))
+    def _():
+        arrived(slow_left, slow_right, deep_pass)
+        derive(jnp.where(slow_right, HALO + planes + NEAR, HALO - NEAR - W2), W2)
+        for t in range(2):
+            arrived(slow_left, slow_right, deep_fields[t])
+            for k in range(1, W1 + 1):
+                advance(t, k, jnp.where(slow_right, EDGE + planes + W1 - k, EDGE - W1 - W2 + k), W2)
 
     crossings = []
     for t in range(2):
-        arrived(second_round[t])
+        arrived(fast_left, fast_right, second_round[t])
         for j in range(1, W2 + 1):
-            advance(t, W1 + j, EDGE - W2 + j, EDGE + planes + W2 - j)
+            advance(t, W1 + j, EDGE - W2 + j, planes + 2 * (W2 - j))
         for p in range(planes):
             totals = accumulate(t, p, W1 + 1, DEGREE + 1, [sums[j, t, p] for j in range(SUMS)])
             out[2 - 2 * core, first + t, p] = totals[0]
@@ -289,21 +309,26 @@
         )
         crossings[t].start()
 
-    everything = [near, far, *first_round, *second_round]
-
-    @pl.when(has_right)
-    def _():
-        for pair in everything:
-            pair[0].wait_send()
-        near_pass[1].wait_send()
-        far_pass[1].wait_send()
-
-    @pl.when(has_left)
-    def _():
-        for pair in everything:
-            pair[1].wait_send()
-        near_pass[0].wait_send()
-        far_pass[0].wait_send()
+    for side, there, fast, slow in ((0, has_right, fast_right, slow_right), (1, has_left, fast_left, slow_left)):
+
+        @pl.when(there)
+        def _():
+            near[side].wait_send()
+            near_pass[1 - side].wait_send()
+            for t in range(2):
+                first_round[t][side].wait_send()
+
+        @pl.when(fast)
+        def _():
+            for t in range(2):
+                second_round[t][side].wait_send()
+
+        @pl.when(slow)
+        def _():
+            deep[side].wait_send()
+            deep_pass[1 - side].wait_send()
+            for t in range(2):
+                deep_fields[t][side].wait_send()
 
     for copy in crossings:
         copy.wait()
@@ -325,8 +350,8 @@
             pltpu.VMEM((2, 3, planes, rows, lanes), jnp.float32),
             pltpu.SMEM((SLICES, LANES), jnp.float32),
             pltpu.SemaphoreType.DMA((4,)),
-            pltpu.SemaphoreType.DMA((2, 6)),
-            pltpu.SemaphoreType.DMA((2, 6)),
+            pltpu.SemaphoreType.DMA((2, 8)),
+            pltpu.SemaphoreType.DMA((2, 8)),
             pltpu.SemaphoreType.DMA((2, 2)),
             pltpu.SemaphoreType.DMA((2, 2)),
             pltpu.SemaphoreType.DMA((2,)),

time: 24 us -> 21.5 us (0.90)
  Pallas kernels: 23 us -> 20.6 us
    pallas_call x1, Pallas kernels: 23 us -> 20.6 us  [body(): pl.pallas_call(functools.partial(kernel, planes), out_shape=jax.ShapeDtyp...]
where the time goes in v4:
time: 21.5 us; the launch traced here: 21.4 us
  Pallas kernels  20.6 us (96%)
  local copies, waits for them, and re-layouts  0.88 us (4%)
    pallas_call x1, Pallas kernels, body(): pl.pallas_call(functools.partial(kernel, planes), out_shape=jax.ShapeDtyp...  20.6 us
    unnamed x1, local copies, waits for them, and re-layouts  0.88 us

profile of v4, /device:TPU:161, one launch (start us, length us, event | category | flops | bytes accessed | tf_op | source)
XLA Modules:
  0.0 21.4 jit_solution(14310626787719233267)
XLA Ops:
  0.0 20.6 %powers.1 = f32[3,4,8,16,128]{4,3,2,1,0:T(8,128)S(1)} custom-call(f32[8,128]{1,0:T(8,128)} %constant.2.clone.weight_rows, f32[4,8,16,128]{3,2,1,0:T(8,128)} %initial.1, f32[3,8,16,128]{3,2,1,0:T(8,128)} %velocity.1, f32[8,16,128]{2,1,0:T(8,128)} %diffusivity.1), custom_call_target="tpu_custom_call" | custom-call | tf_op jit(solution)/shard_map/powers/pallas_call | solution.py:340
  20.6 0.9 %copy.6 = f32[1,3,4,8,16,128]{5,4,3,2,1,0:T(8,128)} copy(f32[1,3,4,8,16,128]{5,4,3,2,1,0:T(8,128)S(1)} %bitcast.1) | data formatting | bytes 1572864

commit v5 on v4

--- a/solution.py
+++ b/solution.py
@@ -76,7 +76,10 @@
 HALO = EDGE - 1
 NEAR = W1 - 1
 SUMS = 5
-GROUP = 16
+ROW = 4
+LAYER = 16
+S1 = 5
+S2 = DEGREE - S1
 LANES = 128
 
 
@@ -92,7 +95,7 @@
     return table
 
 
-def kernel(planes, weight_rows, initial, velocity, diffusivity, out, power, raw, stencil, sums, across, weight,
+def kernel(planes, weight_rows, initial, velocity, diffusivity, out, power, raw, stencil, sums, across, landing, weight,
            local_sem, send, recv, pass_send, pass_recv, cross_send, cross_recv):
     count = lax.axis_size("space")
     me = lax.axis_index("space")
@@ -103,10 +106,17 @@
     has_right = me < count - 1
     left = jnp.maximum(me - 1, 0)
     right = jnp.minimum(me + 1, count - 1)
-    slow_left = jnp.logical_and(has_left, lax.rem(me, GROUP) == 0)
-    slow_right = jnp.logical_and(has_right, lax.rem(me + 1, GROUP) == 0)
-    fast_left = jnp.logical_and(has_left, jnp.logical_not(slow_left))
-    fast_right = jnp.logical_and(has_right, jnp.logical_not(slow_right))
+
+    def kinds(i, there):
+        is_deep = lax.rem(i, LAYER) == 0
+        is_late = jnp.logical_and(lax.rem(i, ROW) == 0, jnp.logical_not(is_deep))
+        is_fast = jnp.logical_not(jnp.logical_or(is_deep, is_late))
+        return [jnp.logical_and(there, kind) for kind in (is_fast, is_late, is_deep)]
+
+    fast_left, late_left, deep_left = kinds(me, has_left)
+    fast_right, late_right, deep_right = kinds(me + 1, has_right)
+    slow_left = jnp.logical_or(late_left, deep_left)
+    slow_right = jnp.logical_or(late_right, deep_right)
     first = 2 * core
     two = pl.ds(first, 2)
     tile = power.shape[3:]
@@ -171,26 +181,47 @@
             device_id_type=MESH,
         )
 
-    near, first_round, second_round, near_pass = [], [[], []], [[], []], []
-    deep, deep_fields, deep_pass = [], [[], []], []
+    def coefficient_halo(side, item, src, dst, width):
+        return remote(side, item, raw.at[two, pl.ds(src, width)], raw.at[two, pl.ds(dst, width)])
+
+    near, near_pass, first_round, second_round = [], [], [[], []], [[], []]
+    near_slow, near_pass_slow, first_slow, second_slow = [], [], [[], []], [[], []]
+    far, far_pass = [], []
+    deep, deep_pass, deep_fields = [], [], [[], []]
+    relay, relay_pass, relay_fields = [], [], [[], []]
     for side in range(2):
-        src = HALO if side else HALO + planes - NEAR
-        dst = HALO + planes if side else HALO - NEAR
-        near.append(remote(side, 0, raw.at[two, pl.ds(src, NEAR)], raw.at[two, pl.ds(dst, NEAR)]))
-        near_pass.append(passed(0, side, dst, NEAR))
+        for width, copies, passes in ((NEAR, near, near_pass), (S1 - 1, near_slow, near_pass_slow)):
+            src = HALO if side else HALO + planes - width
+            dst = HALO + planes if side else HALO - width
+            copies.append(coefficient_halo(side, 0, src, dst, width))
+            passes.append(passed(0, side, dst, width))
+        src = HALO + S1 - 1 if side else HALO + planes - S2 + 1
+        dst = src + planes if side else src - planes
+        far.append(coefficient_halo(side, 1, src, dst, S2 - S1))
+        far_pass.append(passed(1, side, dst, S2 - S1))
+        for width, item, skip, copies, passes in (
+            (planes - S1 + 1, 1, S1 - 1, deep, deep_pass),
+            (DEGREE - 1 - planes, 8, planes, relay, relay_pass),
+        ):
+            src = HALO + skip if side else HALO + planes - skip - width
+            dst = src + planes if side else src - planes
+            copies.append(coefficient_halo(side, item, src, dst, width))
+            passes.append(passed(1 if item == 1 else 2, side, dst, width))
         for t in range(2):
             first_round[t].append(field_halo(side, 2 + t, 0, t, W1))
+            first_slow[t].append(field_halo(side, 2 + t, 0, t, S1))
             second_round[t].append(field_halo(side, 4 + t, W1, t, W2))
-        src = HALO + NEAR if side else HALO + planes - NEAR - W2
-        dst = src + planes if side else src - planes
-        deep.append(remote(side, 1, raw.at[two, pl.ds(src, W2)], raw.at[two, pl.ds(dst, W2)]))
-        deep_pass.append(passed(1, side, dst, W2))
-        src = EDGE + W1 if side else EDGE + planes - W1 - W2
-        dst = src + planes if side else src - planes
-        for t in range(2):
-            deep_fields[t].append(
-                remote(side, 6 + t, power.at[0, t, pl.ds(src, W2)], power.at[0, t, pl.ds(dst, W2)])
-            )
+            src = EDGE if side else EDGE + planes - S2
+            second_slow[t].append(remote(side, 4 + t, power.at[S1, t, pl.ds(src, S2)], landing.at[0, t]))
+            for width, item, skip, copies in (
+                (planes - S1, 4, S1, deep_fields),
+                (DEGREE - planes, 6, planes, relay_fields),
+            ):
+                src = EDGE + skip if side else EDGE + planes - skip - width
+                row = skip - S1 if side else DEGREE - skip - width
+                copies[t].append(
+                    remote(side, item + t, power.at[0, t, pl.ds(src, width)], landing.at[1, t, pl.ds(row, width)])
+                )
 
     def start(to_right, to_left, *pairs):
         for side, there in ((0, to_right), (1, to_left)):
@@ -243,54 +274,101 @@
     derive(HALO, planes)
 
     pl.semaphore_wait(barrier, 1 + has_left.astype(jnp.int32) + has_right.astype(jnp.int32))
-    start(has_right, has_left, near, *first_round)
-
-    for side, there in ((0, slow_right), (1, slow_left)):
+    start(slow_right, slow_left, near_slow, *first_slow)
+    start(fast_right, fast_left, near, *first_round)
+    start(deep_right, deep_left, deep, *deep_fields)
+
+    for side, there in ((0, deep_right), (1, deep_left)):
 
         @pl.when(there)
         def _():
             near[side].wait_recv()
-            deep[side].start()
+            relay[side].start()
             near_pass[side].start()
             for t in range(2):
                 first_round[t][side].wait_recv()
-                deep_fields[t][side].start()
-
-    from_left = jnp.logical_and(has_left, jnp.logical_not(slow_right))
-    from_right = jnp.logical_and(has_right, jnp.logical_not(slow_left))
+                relay_fields[t][side].start()
+
+    from_left = jnp.logical_and(fast_left, jnp.logical_not(deep_right))
+    from_right = jnp.logical_and(fast_right, jnp.logical_not(deep_left))
     arrived(from_left, from_right, near, near_pass)
-    arrived(has_left, has_right, near_pass)
-    derive(HALO - NEAR, NEAR)
-    derive(HALO + planes, NEAR)
+    arrived(slow_left, slow_right, near_slow, near_pass_slow)
+    start(late_right, late_left, far)
+    arrived(fast_left, fast_right, near_pass)
+    arrived(slow_left, slow_right, near_pass_slow)
+    derive(HALO - S1 + 1, S1 - 1)
+    derive(HALO + planes, S1 - 1)
+
+    @pl.when(jnp.logical_not(slow_left))
+    def _():
+        derive(HALO - NEAR, NEAR - S1 + 1)
+
+    @pl.when(jnp.logical_not(slow_right))
+    def _():
+        derive(HALO + planes + S1 - 1, NEAR - S1 + 1)
+
     for t in range(2):
         arrived(from_left, from_right, first_round[t])
+        arrived(slow_left, slow_right, first_slow[t])
         for k in range(1, W1 + 1):
             advance(t, k, EDGE - W1 + k, planes + 2 * (W1 - k))
+            if k == S1:
+                start(late_right, late_left, second_slow[t])
         start(fast_right, fast_left, second_round[t])
 
     for t in range(2):
         for p in range(planes):
-            for j, total in enumerate(accumulate(t, p, 0, W1 + 1, None)):
+            for j, total in enumerate(accumulate(t, p, 0, S1 + 1, None)):
                 sums[j, t, p] = total
 
-    arrived(slow_left, slow_right, deep, deep_pass)
-
-    @pl.when(jnp.logical_or(slow_left, slow_right))
-    def _():
-        arrived(slow_left, slow_right, deep_pass)
-        derive(jnp.where(slow_right, HALO + planes + NEAR, HALO - NEAR - W2), W2)
-        for t in range(2):
-            arrived(slow_left, slow_right, deep_fields[t])
+    arrived(late_left, late_right, far, far_pass)
+    arrived(deep_left, deep_right, deep, deep_pass)
+    arrived(deep_left, deep_right, relay, relay_pass)
+
+    for side, late, far_off in ((0, late_left, deep_left), (1, late_right, deep_right)):
+        for there, arrivals, width in ((late, [far_pass], S2 - S1), (far_off, [deep_pass, relay_pass], S2)):
+
+            @pl.when(there)
+            def _():
+                for passes in arrivals:
+                    passes[side].wait_recv()
+                derive(HALO + planes + S1 - 1 if side else HALO - S1 + 1 - width, width)
+
+    def outer(side, k):
+        return EDGE + planes + S1 - k if side else EDGE - DEGREE + k
+
+    for side, far_off in ((0, deep_left), (1, deep_right)):
+
+        @pl.when(far_off)
+        def _():
+            for t in range(2):
+                deep_fields[t][side].wait_recv()
+                relay_fields[t][side].wait_recv()
+                for i in range(S2):
+                    power[0, t, outer(side, 0) + i] = landing[1, t, i]
             for k in range(1, W1 + 1):
-                advance(t, k, jnp.where(slow_right, EDGE + planes + W1 - k, EDGE - W1 - W2 + k), W2)
+                for t in range(2):
+                    advance(t, k, outer(side, k), S2)
+
+    def widen(t):
+        for side, late in ((0, late_left), (1, late_right)):
+
+            @pl.when(late)
+            def _():
+                second_slow[t][side].wait_recv()
+                for i in range(S2):
+                    power[S1, t, outer(side, S1) + i] = landing[0, t, i]
+                for k in range(S1 + 1, W1 + 1):
+                    advance(t, k, outer(side, k), S2)
 
     crossings = []
     for t in range(2):
+        widen(t)
         arrived(fast_left, fast_right, second_round[t])
         for j in range(1, W2 + 1):
             advance(t, W1 + j, EDGE - W2 + j, planes + 2 * (W2 - j))
         for p in range(planes):
-            totals = accumulate(t, p, W1 + 1, DEGREE + 1, [sums[j, t, p] for j in range(SUMS)])
+            totals = accumulate(t, p, S1 + 1, DEGREE + 1, [sums[j, t, p] for j in range(SUMS)])
             out[2 - 2 * core, first + t, p] = totals[0]
             out[core, first + t, p] = totals[1]
             out[core + 1, first + t, p] = totals[2]
@@ -309,26 +387,24 @@
         )
         crossings[t].start()
 
-    for side, there, fast, slow in ((0, has_right, fast_right, slow_right), (1, has_left, fast_left, slow_left)):
-
-        @pl.when(there)
-        def _():
-            near[side].wait_send()
-            near_pass[1 - side].wait_send()
-            for t in range(2):
-                first_round[t][side].wait_send()
-
-        @pl.when(fast)
-        def _():
-            for t in range(2):
-                second_round[t][side].wait_send()
-
-        @pl.when(slow)
-        def _():
-            deep[side].wait_send()
-            deep_pass[1 - side].wait_send()
-            for t in range(2):
-                deep_fields[t][side].wait_send()
+    sides = (
+        (0, fast_right, slow_right, late_right, deep_right),
+        (1, fast_left, slow_left, late_left, deep_left),
+    )
+    for side, fast, slow, late, far_off in sides:
+        for there, copies, passes in (
+            (fast, [near, *first_round, *second_round], [near_pass]),
+            (slow, [near_slow, *first_slow], [near_pass_slow]),
+            (late, [far, *second_slow], [far_pass]),
+            (far_off, [deep, relay, *deep_fields, *relay_fields], [deep_pass, relay_pass]),
+        ):
+
+            @pl.when(there)
+            def _():
+                for copy in copies:
+                    copy[side].wait_send()
+                for handed in passes:
+                    handed[1 - side].wait_send()
 
     for copy in crossings:
         copy.wait()
@@ -348,12 +424,13 @@
             pltpu.VMEM((7, planes + 2 * HALO, rows, lanes), jnp.float32),
             pltpu.VMEM((SUMS, 2, planes, rows, lanes), jnp.float32),
             pltpu.VMEM((2, 3, planes, rows, lanes), jnp.float32),
+            pltpu.VMEM((2, 2, S2, rows, lanes), jnp.float32),
             pltpu.SMEM((SLICES, LANES), jnp.float32),
             pltpu.SemaphoreType.DMA((4,)),
-            pltpu.SemaphoreType.DMA((2, 8)),
-            pltpu.SemaphoreType.DMA((2, 8)),
-            pltpu.SemaphoreType.DMA((2, 2)),
-            pltpu.SemaphoreType.DMA((2, 2)),
+            pltpu.SemaphoreType.DMA((2, 9)),
+            pltpu.SemaphoreType.DMA((2, 9)),
+            pltpu.SemaphoreType.DMA((3, 2)),
+            pltpu.SemaphoreType.DMA((3, 2)),
             pltpu.SemaphoreType.DMA((2,)),
             pltpu.SemaphoreType.DMA((2,)),
         ],

time: 21.5 us -> 21.3 us (level)
  no operation moved by 1% of the time
where the time goes in v5:
time: 21.3 us
  Pallas kernels  20.4 us (96%)
  local copies, waits for them, and re-layouts  0.88 us (4%)
    pallas_call x1, Pallas kernels, body(): pl.pallas_call(functools.partial(kernel, planes), out_shape=jax.ShapeDtyp...  20.4 us
    unnamed x1, local copies, waits for them, and re-layouts  0.88 us

profile of v5, /device:TPU:161, one launch (start us, length us, event | category | flops | bytes accessed | tf_op | source)
XLA Modules:
  0.0 21.3 jit_solution(15445641787994866499)
XLA Ops:
  0.0 20.4 %powers.1 = f32[3,4,8,16,128]{4,3,2,1,0:T(8,128)S(1)} custom-call(f32[8,128]{1,0:T(8,128)} %constant.2.clone.weight_rows, f32[4,8,16,128]{3,2,1,0:T(8,128)} %initial.1, f32[3,8,16,128]{3,2,1,0:T(8,128)} %velocity.1, f32[8,16,128]{2,1,0:T(8,128)} %diffusivity.1), custom_call_target="tpu_custom_call" | custom-call | tf_op jit(solution)/shard_map/powers/pallas_call | solution.py:416
  20.4 0.9 %copy.6 = f32[1,3,4,8,16,128]{5,4,3,2,1,0:T(8,128)} copy(f32[1,3,4,8,16,128]{5,4,3,2,1,0:T(8,128)S(1)} %bitcast.1) | data formatting | bytes 1572864

commit v6 on v5

--- a/solution.py
+++ b/solution.py
@@ -276,18 +276,29 @@
     pl.semaphore_wait(barrier, 1 + has_left.astype(jnp.int32) + has_right.astype(jnp.int32))
     start(slow_right, slow_left, near_slow, *first_slow)
     start(fast_right, fast_left, near, *first_round)
-    start(deep_right, deep_left, deep, *deep_fields)
+
+    @pl.when(deep_right)
+    def _():
+        deep[0].start()
+        deep_fields[0][0].start()
 
     for side, there in ((0, deep_right), (1, deep_left)):
 
         @pl.when(there)
         def _():
             near[side].wait_recv()
+            near_pass[side].start()
+            if side:
+                deep[side].start()
+                deep_fields[0][side].start()
             relay[side].start()
-            near_pass[side].start()
-            for t in range(2):
-                first_round[t][side].wait_recv()
-                relay_fields[t][side].start()
+            first_round[0][side].wait_recv()
+            relay_fields[0][side].start()
+            first_round[1][side].wait_recv()
+            if not side:
+                relay_fields[0][side].wait_send()
+                deep_fields[1][side].start()
+                relay_fields[1][side].start()
 
     from_left = jnp.logical_and(fast_left, jnp.logical_not(deep_right))
     from_right = jnp.logical_and(fast_right, jnp.logical_not(deep_left))
@@ -315,6 +326,13 @@
             if k == S1:
                 start(late_right, late_left, second_slow[t])
         start(fast_right, fast_left, second_round[t])
+        if t == 0:
+
+            @pl.when(deep_left)
+            def _():
+                deep_fields[1][1].start()
+                relay_fields[1][1].start()
+
 
     for t in range(2):
         for p in range(planes):
@@ -337,21 +355,17 @@
     def outer(side, k):
         return EDGE + planes + S1 - k if side else EDGE - DEGREE + k
 
-    for side, far_off in ((0, deep_left), (1, deep_right)):
-
-        @pl.when(far_off)
-        def _():
-            for t in range(2):
+    def widen(t):
+        for side, late, far_off in ((0, late_left, deep_left), (1, late_right, deep_right)):
+
+            @pl.when(far_off)
+            def _():
                 deep_fields[t][side].wait_recv()
                 relay_fields[t][side].wait_recv()
                 for i in range(S2):
                     power[0, t, outer(side, 0) + i] = landing[1, t, i]
-            for k in range(1, W1 + 1):
-                for t in range(2):
+                for k in range(1, W1 + 1):
                     advance(t, k, outer(side, k), S2)
-
-    def widen(t):
-        for side, late in ((0, late_left), (1, late_right)):
 
             @pl.when(late)
             def _():
@@ -402,7 +416,8 @@
             @pl.when(there)
             def _():
                 for copy in copies:
-                    copy[side].wait_send()
+                    if side or copy is not relay_fields[0]:
+                        copy[side].wait_send()
                 for handed in passes:
                     handed[1 - side].wait_send()
 

time: 21.3 us -> 21.2 us (level)
  no operation moved by 1% of the time
where the time goes in v6:
time: 21.2 us; the launch traced here: 21.1 us
  Pallas kernels  20.2 us (95%)
  local copies, waits for them, and re-layouts  0.88 us (4%)
    pallas_call x1, Pallas kernels, body(): pl.pallas_call(functools.partial(kernel, planes), out_shape=jax.ShapeDtyp...  20.2 us
    unnamed x1, local copies, waits for them, and re-layouts  0.88 us

profile of v6, /device:TPU:161, one launch (start us, length us, event | category | flops | bytes accessed | tf_op | source)
XLA Modules:
  0.0 21.1 jit_solution(14829120812077307152)
XLA Ops:
  0.0 20.2 %powers.1 = f32[3,4,8,16,128]{4,3,2,1,0:T(8,128)S(1)} custom-call(f32[8,128]{1,0:T(8,128)} %constant.2.clone.weight_rows, f32[4,8,16,128]{3,2,1,0:T(8,128)} %initial.1, f32[3,8,16,128]{3,2,1,0:T(8,128)} %velocity.1, f32[8,16,128]{2,1,0:T(8,128)} %diffusivity.1), custom_call_target="tpu_custom_call" | custom-call | tf_op jit(solution)/shard_map/powers/pallas_call | solution.py:431
  20.2 0.9 %copy.6 = f32[1,3,4,8,16,128]{5,4,3,2,1,0:T(8,128)} copy(f32[1,3,4,8,16,128]{5,4,3,2,1,0:T(8,128)S(1)} %bitcast.1) | data formatting | bytes 1572864

commit v7 on v6

--- a/solution.py
+++ b/solution.py
@@ -334,14 +334,14 @@
                 relay_fields[1][1].start()
 
 
+    arrived(late_left, late_right, far, far_pass)
+    arrived(deep_left, deep_right, deep, deep_pass)
+    arrived(deep_left, deep_right, relay, relay_pass)
+
     for t in range(2):
         for p in range(planes):
             for j, total in enumerate(accumulate(t, p, 0, S1 + 1, None)):
                 sums[j, t, p] = total
-
-    arrived(late_left, late_right, far, far_pass)
-    arrived(deep_left, deep_right, deep, deep_pass)
-    arrived(deep_left, deep_right, relay, relay_pass)
 
     for side, late, far_off in ((0, late_left, deep_left), (1, late_right, deep_right)):
         for there, arrivals, width in ((late, [far_pass], S2 - S1), (far_off, [deep_pass, relay_pass], S2)):

time: 21.2 us -> 21.2 us (level)
  no operation moved by 1% of the time
where the time goes in v7:
time: 21.2 us; the launch traced here: 21.1 us
  Pallas kernels  20.2 us (95%)
  local copies, waits for them, and re-layouts  0.88 us (4%)
    pallas_call x1, Pallas kernels, body(): pl.pallas_call(functools.partial(kernel, planes), out_shape=jax.ShapeDtyp...  20.2 us
    unnamed x1, local copies, waits for them, and re-layouts  0.88 us

profile of v7, /device:TPU:161, one launch (start us, length us, event | category | flops | bytes accessed | tf_op | source)
XLA Modules:
  0.0 21.1 jit_solution(11755613815121442430)
XLA Ops:
  0.0 20.2 %powers.1 = f32[3,4,8,16,128]{4,3,2,1,0:T(8,128)S(1)} custom-call(f32[8,128]{1,0:T(8,128)} %constant.2.clone.weight_rows, f32[4,8,16,128]{3,2,1,0:T(8,128)} %initial.1, f32[3,8,16,128]{3,2,1,0:T(8,128)} %velocity.1, f32[8,16,128]{2,1,0:T(8,128)} %diffusivity.1), custom_call_target="tpu_custom_call" | custom-call | tf_op jit(solution)/shard_map/powers/pallas_call | solution.py:431
  20.2 0.9 %copy.6 = f32[1,3,4,8,16,128]{5,4,3,2,1,0:T(8,128)} copy(f32[1,3,4,8,16,128]{5,4,3,2,1,0:T(8,128)S(1)} %bitcast.1) | data formatting | bytes 1572864
